TPU v7x, 256 devices: a whole 4x4x8 slice. The times are simulated.
256 devices in a mesh: replica: 4 (over x), fsdp: 32 (over y_hi, z, core), tensor: 2 (over y_lo).
Axes of the slice: x: 4, y: 4 (y_hi: 2, y_lo: 2; y = y_hi * 2 + y_lo), z: 8, core: 2. Of those that a mesh axis runs over, the one named last changes fastest.
Arguments:
- tokens: bfloat16 [4, 16384, 8192], P('replica', 'fsdp'), may hold values from -6 to 6
- pseudo_grad: bfloat16 [4, 8192, 1024], P('replica', 'fsdp', 'tensor'), may hold values from -0.078125 to 0.078125
- anchor: float32 [8192, 2, 4, 128], P('fsdp', 'tensor', 'replica'), may hold values from -0.0625 to 0.0625
- momentum: float32 [8192, 2, 4, 128], P('fsdp', 'tensor', 'replica'), may hold values from -0.0625 to 0.0625
Outputs:
- keys: bfloat16 [4, 16384, 1024], P('replica', 'fsdp', 'tensor')
- anchor_new: float32 [8192, 2, 4, 128], P('fsdp', 'tensor', 'replica')
- momentum_new: float32 [8192, 2, 4, 128], P('fsdp', 'tensor', 'replica')
All inputs are finite; a program needn't handle non-finite values.
Results may differ from a plain program's by a relative error of at most 0.015.
Values may be sent and summed in bfloat16 or wider, within the bound.
No kernel may reach another device: no remote copies, remote signals or barrier semaphores. Data moves between devices by JAX's collectives and lax.ppermute only.
A program may use at most 64 MiB of HBM per device.

v0:
```python
import jax
import jax.numpy as jnp
from jax import lax
from jax.sharding import PartitionSpec as P

outer_rate = 0.7
momentum_keep = 0.9


def per_device(tokens, pseudo_grad, anchor, momentum):
    local_rows = pseudo_grad.shape[1]
    block_width = anchor.shape[3]
    islands = lax.axis_size("replica")
    grouped = pseudo_grad[0].astype(jnp.float32).reshape(local_rows, islands, block_width)
    summed = lax.psum_scatter(
        grouped.astype(jnp.bfloat16), "replica", scatter_dimension=1, tiled=True
    ).astype(jnp.float32)
    delta = (summed * (1.0 / islands)).reshape(anchor.shape)
    momentum_new = momentum_keep * momentum + delta
    anchor_new = anchor - outer_rate * (delta + momentum_keep * momentum_new)
    piece = anchor_new.astype(jnp.bfloat16).reshape(local_rows, block_width)
    hidden = tokens[0]
    wide = lax.all_gather(piece, "replica", axis=1, tiled=True)
    result = jnp.dot(
        hidden, lax.all_gather(wide, "fsdp", axis=0, tiled=True), preferred_element_type=jnp.float32
    )
    keys = result.astype(jnp.bfloat16)[None]
    return (keys, anchor_new, momentum_new)


def solution(mesh):
    return jax.shard_map(
        per_device,
        mesh=mesh,
        in_specs=(
            P("replica", "fsdp", None),
            P("replica", "fsdp", "tensor"),
            P("fsdp", "tensor", "replica", None),
            P("fsdp", "tensor", "replica", None),
        ),
        out_specs=(
            P("replica", "fsdp", "tensor"),
            P("fsdp", "tensor", "replica", None),
            P("fsdp", "tensor", "replica", None),
        ),
        check_vma=False,
    )
```

profile of v0, /device:TPU:1, one launch (start us, length us, event | category | flops | bytes accessed | tf_op | source)
XLA Modules:
  0.0 178.8 jit_solution(5882427292587224606)
XLA Ops:
  7.2 0.0 reduce-scatter.2.cloned.1.call-start
  7.2 1.8 %copy.8 = bf16[1,256,512]{1,2,0:T(8,128)(2,1)} copy(bf16[1,256,512]{2,1,0:T(8,128)(2,1)} %param.5) | data formatting | bytes 524288 | tf_op args[1]
  9.0 0.0 reduce-scatter.2.cloned.1.call-update
  9.0 0.0 all-gather.4.cloned.1.call-start
  9.1 1.0 copy.10
  10.1 1.0 copy.9
  11.1 24.7 %reduce-scatter.2.cloned.1.call-done = bf16[256,1,128]{0,2,1:T(8,128)(2,1)} async-done(((bf16[256,4,128]{0,2,1:T(8,128)(2,1)}), bf16[256,1,128]{0,2,1:T(8,128)(2,1)}) %reduce-scatter.2.cloned.1.call-update) | async-done | bytes 65552 | tf_op jit(solution)/shard_map/reduce_scatter | solution.py:15
  35.8 0.9 fusion.15
  36.7 11.0 %all-gather = bf16[256,1,1,512]{0,3,2,1:T(8,128)(2,1)} all-gather(bf16[256,1,1,128]{0,3,2,1:T(8,128)(2,1)S(1)} %get-tuple-element.9), channel_id=2, replica_groups=mesh['replica'=4,'fsdp'=32,'tensor'=2] {'replica'}, dimensions={3}, use_global_device_ids=true | all-gather | bytes 327680 | tf_op jit(solution)/shard_map/all_gather | solution.py:23
  47.7 0.0 all-gather.4.cloned.1.call-update
  47.7 0.8 copy.12
  48.5 0.8 copy.13
  49.3 111.4 %all-gather.4.cloned.1.call-done = bf16[8192,1,1,512]{0,3,2,1:T(8,128)(2,1)} async-done(((bf16[256,1,1,512]{0,3,2,1:T(8,128)(2,1)}), bf16[8192,1,1,512]{0,3,2,1:T(8,128)(2,1)}) %all-gather.4.cloned.1.call-update) | async-done | bytes 8388624 | tf_op jit(solution)/shard_map/all_gather | solution.py:25
  160.7 10.3 %fusion.8 = bf16[1,512,512]{1,2,0:T(8,128)(2,1)S(1)} fusion(bf16[1,512,8192]{2,1,0:T(8,128)(2,1)} %param.4, bf16[8192,1,1,512]{0,3,2,1:T(8,128)(2,1)} %all-gather.4.cloned.1.call-done), kind=kOutput, calls=%fused_computation.4 | convolution fusion | flops 4295229440 | bytes 17301504 | tf_op jit(solution)/shard_map/dot_general | solution.py:24
  170.9 1.0 copy.11
Async XLA Ops:
  7.2 28.6 %reduce-scatter.2.cloned.1.call-start = ((), (), s32[]{:S(2)}) async-start(), calls=%async_computation.1 | async-start | bytes 327680 | tf_op jit(solution)/shard_map/reduce_scatter | solution.py:15
  9.0 151.6 %all-gather.4.cloned.1.call-start = ((), (), s32[]{:S(2)}) async-start(), calls=%async_computation.2 | async-start | bytes 8650752 | tf_op jit(solution)/shard_map/all_gather | solution.py:25
Sparse Core Ops, SparseCore 0:
  11.1 24.6 reduce-scatter.1
  47.9 112.7 all-gather.3
where the time goes:
time: 179 us
  waiting for transfers between devices  136 us (76%)
  between operations  14.1 us (8%)
  blocking collectives  11 us (6%)
  matrix products  10.3 us (6%)
  local copies, waits for them, and re-layouts  6.31 us (4%)
    all_gather x1, waiting for transfers between devices, per_device(): lax.all_gather(wide, 'fsdp', axis=0, tiled=True)  111 us
    reduce_scatter x1, waiting for transfers between devices, per_device(): lax.psum_scatter(grouped.astype(jnp.bfloat16), 'replica', scatter_dimensi...  24.7 us
    all_gather x1, blocking collectives, per_device(): wide = lax.all_gather(piece, 'replica', axis=1, tiled=True)  11 us
    dot_general x1, matrix products, per_device(): jnp.dot(hidden, lax.all_gather(wide, 'fsdp', axis=0, tiled=True), preferr...  10.3 us
    unnamed x6, local copies, waits for them, and re-layouts  6.31 us
  transfers between devices with their start and end apart: 2, of which 2 were waited for; matrix products, arithmetic and copies ran while one was open for 2% of the time, Pallas kernels for 0%

commit v1 on v0

v1 whole, which is shorter than its diff:
```python
import functools

import jax
import jax.numpy as jnp
from jax import lax
from jax.experimental import pallas as pl
from jax.experimental.pallas import tpu as pltpu
from jax.sharding import PartitionSpec as P

outer_rate = 0.7
momentum_keep = 0.9

AXES = ("replica", "fsdp", "tensor")
STEPS = (1, -1, 2)
VMEM_LIMIT = 48 * 1024 * 1024


def pairs(move):
    out = []
    for x in range(4):
        for y in range(2):
            for z in range(8):
                for c in range(2):
                    for t in range(2):
                        to_x, to_y, to_z, to_c = move(x, y, z, c)
                        source = (x * 32 + y * 16 + z * 2 + c) * 2 + t
                        target = ((to_x % 4) * 32 + (to_y % 2) * 16 + (to_z % 8) * 2 + to_c % 2) * 2 + t
                        out.append((source, target))
    return out


def send(value, move):
    return lax.ppermute(value, AXES, pairs(move))


def along_x(step):
    return lambda x, y, z, c: (x + step, y, z, c)


def early(step):
    return lambda x, y, z, c: (x + step, y, z, c) if c == 0 else (x, y, z + step, c)


def late(step):
    return lambda x, y, z, c: (x, y, z + step, c) if c == 0 else (x + step, y, z, c)


def position():
    index = lax.axis_index("fsdp")
    return lax.axis_index("replica"), index // 16, (index // 2) % 8, index % 2


def wrap(value):
    return lax.rem(value + 4, 4)


def call(kernel, out_shape, *, flops=0, size=1, scratch=(), in_specs=None):
    specs = {} if in_specs is None else {"in_specs": in_specs}
    return pl.pallas_call(
        kernel,
        out_shape=out_shape,
        **specs,
        scratch_shapes=list(scratch),
        compiler_params=pltpu.CompilerParams(vmem_limit_bytes=VMEM_LIMIT),
        cost_estimate=pl.CostEstimate(flops=flops, bytes_accessed=size, transcendentals=0),
    )


def split_kernel(grad, *outs):
    x, _, _, _ = position()
    for step, out in zip((0,) + STEPS, outs):
        first = pl.multiple_of(wrap(x + step) * 128, 128)
        out[...] = grad[:, pl.ds(first, 128)]


def update_kernel(own, one, two, three, anchor, momentum, anchor_new, momentum_new, weights):
    total = own[...].astype(jnp.float32) + one[...].astype(jnp.float32)
    total = total + (two[...].astype(jnp.float32) + three[...].astype(jnp.float32))
    delta = total * 0.25
    kept = momentum_keep * momentum[...] + delta
    moved = anchor[...] - outer_rate * (delta + momentum_keep * kept)
    momentum_new[...] = kept
    anchor_new[...] = moved
    weights[...] = moved.astype(jnp.bfloat16)


def join_pairs_kernel(own, by_y, by_z, by_both, out):
    _, y, z, _ = position()
    here = y * 2 + z // 4
    other_y, other_z = 1 - y, 1 - z // 4
    out[here] = own[...]
    out[other_y * 2 + z // 4] = by_y[...]
    out[y * 2 + other_z] = by_z[...]
    out[other_y * 2 + other_z] = by_both[...]


def join_four_kernel(own, one, two, three, out):
    x, _, z, c = position()
    here = jnp.where(c == 0, x, z % 4)
    for step, piece in zip((0,) + STEPS, (own, one, two, three)):
        out[pl.ds(wrap(here - step) * 4, 4)] = piece[...]


def pack_kernel(own, other, out, sems):
    _, _, _, c = position()
    copies = []
    for side, tokens in enumerate((own, other)):
        for near in range(4):
            for pair in range(4):
                row = (pair // 2) * 16 + ((pair % 2) * 4 + near) * 2
                source = pl.multiple_of((row + c) * 256, 256)
                copies.append(
                    pltpu.make_async_copy(
                        tokens.at[:, pl.ds(source, 256)],
                        out.at[pl.ds(side * 512, 512), pl.ds((near * 4 + pair) * 256, 256)],
                        sems.at[len(copies)],
                    )
                )
    for copy in copies:
        copy.start()
    for copy in copies:
        copy.wait()


def product_kernel(steps, first_row, rows, has_start, packed, left, right, *rest):
    start, out = (rest[0], rest[1]) if has_start else (None, rest[0])
    x, _, z, c = position()
    tile = 256

    @pl.when(c == 0)
    def _():
        @pl.loop(0, rows // tile)
        def _(m):
            here = pl.ds(pl.multiple_of(m * tile, tile), tile)
            there = pl.ds(pl.multiple_of(first_row + m * tile, tile), tile)
            for half in range(2):
                columns = pl.ds(half * 256, 256)
                total = start[here, columns] if has_start else None
                for step, piece in zip(steps, (left, right)):
                    near = pl.multiple_of(wrap(z % 4 - step) * 1024, 1024)
                    block = jnp.concatenate(
                        [piece[pl.ds((half * 2 + q) * 4, 4)].reshape(1024, 128) for q in range(2)], axis=1
                    )
                    term = jnp.dot(packed[there, pl.ds(near, 1024)], block, preferred_element_type=jnp.float32)
                    total = term if total is None else total + term
                out[here, columns] = total

    @pl.when(c == 1)
    def _():
        @pl.loop(0, rows // tile)
        def _(m):
            here = pl.ds(pl.multiple_of(m * tile, tile), tile)
            there = pl.ds(pl.multiple_of(first_row + m * tile, tile), tile)
            block = jnp.concatenate([left[...].reshape(4096, 128), right[...].reshape(4096, 128)], axis=1)
            term = jnp.dot(packed[there, :], block, preferred_element_type=jnp.float32)
            if has_start:
                out[here, :] = start[here, :]
            for k, step in enumerate(steps):
                column = pl.multiple_of(wrap(x - step) * 128, 128)
                out[here, pl.ds(column, 128)] = term[:, k * 128 : (k + 1) * 128]


def product(packed, left, right, steps, first_row, rows, start=None):
    args = (packed, left, right) + (() if start is None else (start,))
    return call(
        functools.partial(product_kernel, steps, first_row, rows, start is not None),
        jax.ShapeDtypeStruct((rows, 512), jnp.float32),
        flops=2 * rows * 2048 * 512,
        size=rows * 8192 + 2 * 2**20,
    )(*args)


def per_device(tokens, pseudo_grad, anchor, momentum):
    block = jax.ShapeDtypeStruct((256, 128), jnp.bfloat16)
    state = jax.ShapeDtypeStruct((256, 128), jnp.float32)
    own_tokens = tokens[0]
    grads = call(split_kernel, (block,) * 4, size=2**19)(pseudo_grad[0])
    arrived = [send(grads[k + 1], along_x(step)) for k, step in enumerate(STEPS)]
    other_tokens = send(own_tokens, lambda x, y, z, c: (x, y, z, c + 1))
    anchor_new, momentum_new, weights = call(update_kernel, (state, state, block), size=2**20)(
        grads[0], *arrived, anchor.reshape(256, 128), momentum.reshape(256, 128)
    )
    swaps = [
        send(weights, lambda x, y, z, c: (x, y + 1, z, c)),
        send(weights, lambda x, y, z, c: (x, y, z + 4, c)),
        send(weights, lambda x, y, z, c: (x, y + 1, z + 4, c)),
    ]
    four = call(join_pairs_kernel, jax.ShapeDtypeStruct((4, 256, 128), jnp.bfloat16), size=2**19)(weights, *swaps)
    fours = [send(four, early(step)) for step in STEPS]
    mine = call(join_four_kernel, jax.ShapeDtypeStruct((16, 256, 128), jnp.bfloat16), size=2**21)(four, *fours)
    packed = call(
        pack_kernel,
        jax.ShapeDtypeStruct((1024, 4096), jnp.bfloat16),
        size=2**24,
        scratch=(pltpu.SemaphoreType.DMA((32,)),),
        in_specs=[pl.BlockSpec(memory_space=pl.ANY)] * 2,
    )(own_tokens, other_tokens)
    far = {step: send(mine, late(step)) for step in STEPS}
    first = product(packed, mine, far[1], (0, 1), 0, 1024)
    away = product(packed, far[-1], far[2], (-1, 2), 512, 512, first[512:])
    returned = send(away.astype(jnp.bfloat16), lambda x, y, z, c: (x, y, z, c + 1))
    here = product(packed, far[-1], far[2], (-1, 2), 0, 512, first[:512])
    keys = (here + returned.astype(jnp.float32)).astype(jnp.bfloat16)[None]
    return keys, anchor_new.reshape(anchor.shape), momentum_new.reshape(momentum.shape)


def solution(mesh):
    return jax.shard_map(
        per_device,
        mesh=mesh,
        in_specs=(
            P("replica", "fsdp", None),
            P("replica", "fsdp", "tensor"),
            P("fsdp", "tensor", "replica", None),
            P("fsdp", "tensor", "replica", None),
        ),
        out_specs=(
            P("replica", "fsdp", "tensor"),
            P("fsdp", "tensor", "replica", None),
            P("fsdp", "tensor", "replica", None),
        ),
        check_vma=False,
    )
```

time: 179 us -> 96 us (0.54)
  waiting for transfers between devices: 136 us -> 31.3 us
  starting transfers between devices: 0.08 us -> 32.7 us
  Pallas kernels: 0 us -> 23.8 us
  between operations: 14.1 us -> 0.73 us
  blocking collectives: 11 us -> 0 us
  matrix products: 10.3 us -> 0 us
    all_gather x1 -> x0, waiting for transfers between devices: 111 us -> none  [per_device(): lax.all_gather(wide, 'fsdp', axis=0, tiled=True)]
    ppermute x0 -> x14, starting transfers between devices: none -> 32.7 us  [send(): return lax.ppermute(value, AXES, pairs(move))]
    ppermute x0 -> x14, waiting for transfers between devices: none -> 31.3 us  [send(): return lax.ppermute(value, AXES, pairs(move))]
    reduce_scatter x1 -> x0, waiting for transfers between devices: 24.7 us -> none  [per_device(): lax.psum_scatter(grouped.astype(jnp.bfloat16), 'replica', scatter_dimensi...]
    pallas_call x0 -> x8, Pallas kernels: none -> 23.8 us  [the longest x3 15.9 us: product(): call(functools.partial(product_kernel, steps, first_row, rows, start is n...]
    all_gather x1 -> x0, blocking collectives: 11 us -> none  [per_device(): wide = lax.all_gather(piece, 'replica', axis=1, tiled=True)]
    dot_general x1 -> x0, matrix products: 10.3 us -> none  [per_device(): jnp.dot(hidden, lax.all_gather(wide, 'fsdp', axis=0, tiled=True), preferr...]
    unnamed x6 -> x8, local copies, waits for them, and re-layouts: 6.31 us -> 5.99 us
  transfers between devices with their start and end apart: 2 -> 14, of which waited for: 2 -> 10; matrix products, arithmetic and copies ran while one was open for 2% -> 0% of each run, Pallas kernels for 0% -> 20%
where the time goes in v1:
time: 96 us; the launch traced here: 95.7 us
  starting transfers between devices  32.7 us (34%)
  waiting for transfers between devices  31.3 us (33%)
  Pallas kernels  23.8 us (25%)
  local copies, waits for them, and re-layouts  6.16 us (6%)
  other arithmetic  1.02 us (1%)
    ppermute x14, starting transfers between devices, send(): return lax.ppermute(value, AXES, pairs(move))  32.7 us
    ppermute x14, waiting for transfers between devices, send(): return lax.ppermute(value, AXES, pairs(move))  31.3 us
    pallas_call x3, Pallas kernels, product(): call(functools.partial(product_kernel, steps, first_row, rows, start is n...  15.9 us
    pallas_call x1, Pallas kernels, per_device(): call(pack_kernel, jax.ShapeDtypeStruct((1024, 4096), jnp.bfloat16), size=...  6.99 us
    unnamed x8, local copies, waits for them, and re-layouts  5.99 us
  transfers between devices with their start and end apart: 14, of which 10 were waited for; matrix products, arithmetic and copies ran while one was open for 0% of the time, Pallas kernels for 20%

profile of v1, /device:TPU:1, one launch (start us, length us, event | category | flops | bytes accessed | tf_op | source)
XLA Modules:
  0.0 95.7 jit_solution(9519733963176327182)
XLA Ops:
  0.6 3.3 %collective-permute-start = (bf16[512,8192]{1,0:T(8,128)(2,1)}, bf16[512,8192]{1,0:T(8,128)(2,1)S(1)}, u32[]{:S(2)}, u32[]{:S(2)}) collective-permute-start(bf16[512,8192]{1,0:T(8,128)(2,1)} %bitcast.15), channel_id=1, source_target_pairs={{0,2},{1,3},{2,0},{3,1},{4,6},{5,7},{6,4},{7,5},{8,10},{9,11},{10,... | collective-permute-start | bytes 25165832 | tf_op jit(solution)/shard_map/ppermute | solution.py:33
  4.0 0.0 copy-start
  4.0 0.9 copy-done
  5.0 0.1 collective-permute-start.1
  5.1 2.7 %collective-permute-start.2 = (bf16[256,128]{1,0:T(8,128)(2,1)S(1)}, bf16[256,128]{1,0:T(8,128)(2,1)S(1)}, u32[]{:S(2)}, u32[]{:S(2)}) collective-permute-start(bf16[256,128]{1,0:T(8,128)(2,1)S(1)} %get-tuple-element.12), channel_id=1, source_target_pairs={{0,192},{1,193},{2,194},{3,195},{4,196},{5,197},{6,198},{7,199},{8... | collective-permute-start | bytes 196616 | tf_op jit(solution)/shard_map/ppermute | solution.py:33
  7.7 0.0 collective-permute-start.3
  7.7 2.2 %collective-permute-done.1.one = bf16[256,128]{1,0:T(8,128)(2,1)S(1)} collective-permute-done((bf16[256,128]{1,0:T(8,128)(2,1)S(1)}, bf16[256,128]{1,0:T(8,128)(2,1)S(1)}, u32[]{:S(2)}, u32[]{:S(2)}) %collective-permute-start.1) | collective-permute-done | bytes 65568 | tf_op jit(solution)/shard_map/ppermute | solution.py:33
  10.0 0.6 collective-permute-done.2.two
  10.5 1.8 %collective-permute-done.3.three = bf16[256,128]{1,0:T(8,128)(2,1)S(1)} collective-permute-done((bf16[256,128]{1,0:T(8,128)(2,1)S(1)}, bf16[256,128]{1,0:T(8,128)(2,1)S(1)}, u32[]{:S(2)}, u32[]{:S(2)}) %collective-permute-start.3) | collective-permute-done | bytes 65568 | tf_op jit(solution)/shard_map/ppermute | solution.py:33
  12.3 0.0 copy-start.1
  12.3 0.9 copy-done.1
  13.2 0.0 copy-start.2
  13.2 0.9 copy-done.2
  14.1 0.7 shard_map.69
  14.9 1.2 %collective-permute-start.4 = (bf16[256,128]{1,0:T(8,128)(2,1)S(1)}, bf16[256,128]{1,0:T(8,128)(2,1)S(1)}, u32[]{:S(2)}, u32[]{:S(2)}) collective-permute-start(bf16[256,128]{1,0:T(8,128)(2,1)S(1)} %get-tuple-element.14.own), channel_id=1, source_target_pairs={{0,32},{1,33},{2,34},{3,35},{4,36},{5,37},{6,38},{7,39},{8,40},{9,... | collective-permute-start | bytes 196616 | tf_op jit(solution)/shard_map/ppermute | solution.py:33
  16.1 6.9 %collective-permute-start.5 = (bf16[256,128]{1,0:T(8,128)(2,1)S(1)}, bf16[256,128]{1,0:T(8,128)(2,1)S(1)}, u32[]{:S(2)}, u32[]{:S(2)}) collective-permute-start(bf16[256,128]{1,0:T(8,128)(2,1)S(1)} %get-tuple-element.14.own), channel_id=1, source_target_pairs={{0,16},{1,17},{2,18},{3,19},{4,20},{5,21},{6,22},{7,23},{8,24},{9,... | collective-permute-start | bytes 196616 | tf_op jit(solution)/shard_map/ppermute | solution.py:33
  23.0 0.0 collective-permute-start.6
  23.0 0.0 collective-permute-done.4.by_y
  23.0 1.7 %collective-permute-done.5.by_z = bf16[256,128]{1,0:T(8,128)(2,1)S(1)} collective-permute-done((bf16[256,128]{1,0:T(8,128)(2,1)S(1)}, bf16[256,128]{1,0:T(8,128)(2,1)S(1)}, u32[]{:S(2)}, u32[]{:S(2)}) %collective-permute-start.5) | collective-permute-done | bytes 65568 | tf_op jit(solution)/shard_map/ppermute | solution.py:33
  24.7 7.7 %collective-permute-done.6.by_both = bf16[256,128]{1,0:T(8,128)(2,1)S(1)} collective-permute-done((bf16[256,128]{1,0:T(8,128)(2,1)S(1)}, bf16[256,128]{1,0:T(8,128)(2,1)S(1)}, u32[]{:S(2)}, u32[]{:S(2)}) %collective-permute-start.6) | collective-permute-done | bytes 65568 | tf_op jit(solution)/shard_map/ppermute | solution.py:33
  32.5 0.9 collective-permute-start.7
  33.4 1.8 %collective-permute-start.8 = (bf16[4,256,128]{2,1,0:T(8,128)(2,1)S(1)}, bf16[4,256,128]{2,1,0:T(8,128)(2,1)S(1)}, u32[]{:S(2)}, u32[]{:S(2)}) collective-permute-start(bf16[4,256,128]{2,1,0:T(8,128)(2,1)S(1)} %shard_map.70.own), channel_id=1, source_target_pairs={{0,192},{1,193},{2,30},{3,31},{4,196},{5,197},{6,2},{7,3},{8,200},... | collective-permute-start | bytes 786440 | tf_op jit(solution)/shard_map/ppermute | solution.py:33
  35.2 0.0 collective-permute-start.9
  35.2 3.8 %collective-permute-done.7.one = bf16[4,256,128]{2,1,0:T(8,128)(2,1)S(1)} collective-permute-done((bf16[4,256,128]{2,1,0:T(8,128)(2,1)S(1)}, bf16[4,256,128]{2,1,0:T(8,128)(2,1)S(1)}, u32[]{:S(2)}, u32[]{:S(2)}) %collective-permute-start.7) | collective-permute-done | bytes 262176 | tf_op jit(solution)/shard_map/ppermute | solution.py:33
  39.0 0.0 collective-permute-done.8.two
  39.0 6.7 %collective-permute-done.9.three = bf16[4,256,128]{2,1,0:T(8,128)(2,1)S(1)} collective-permute-done((bf16[4,256,128]{2,1,0:T(8,128)(2,1)S(1)}, bf16[4,256,128]{2,1,0:T(8,128)(2,1)S(1)}, u32[]{:S(2)}, u32[]{:S(2)}) %collective-permute-start.9) | collective-permute-done | bytes 262176 | tf_op jit(solution)/shard_map/ppermute | solution.py:33
  45.7 0.1 shard_map.71.left
  45.8 0.1 collective-permute-start.12
  45.9 2.6 %collective-permute-start.10 = (bf16[16,256,128]{2,1,0:T(8,128)(2,1)S(1)}, bf16[16,256,128]{2,1,0:T(8,128)(2,1)S(1)}, u32[]{:S(2)}, u32[]{:S(2)}) collective-permute-start(bf16[16,256,128]{2,1,0:T(8,128)(2,1)S(1)} %shard_map.71.left), channel_id=1, source_target_pairs={{0,28},{1,29},{2,194},{3,195},{4,0},{5,1},{6,198},{7,199},{8,4},{9... | collective-permute-start | bytes 3145736 | tf_op jit(solution)/shard_map/ppermute | solution.py:33
  48.5 0.2 collective-permute-start.11
  48.7 0.0 collective-permute-done.other
  48.7 0.0 copy-start.3
  48.7 3.2 %copy-done.3 = bf16[512,8192]{1,0:T(8,128)(2,1)} copy-done((bf16[512,8192]{1,0:T(8,128)(2,1)}, bf16[512,8192]{1,0:T(8,128)(2,1)S(1)}, u32[]{:S(2)}) %copy-start.3) | copy-done | bytes 8388632
  51.9 7.0 %shard_map.67.packed = bf16[1024,4096]{1,0:T(8,128)(2,1)} custom-call(bf16[512,8192]{1,0:T(8,128)(2,1)} %bitcast.16, bf16[512,8192]{1,0:T(8,128)(2,1)} %copy-done.3), custom_call_target="tpu_custom_call" | custom-call | bytes 16777216 | tf_op jit(solution)/shard_map/pallas_call | solution.py:191
  58.9 2.1 %collective-permute-done.12.right = bf16[16,256,128]{2,1,0:T(8,128)(2,1)S(1)} collective-permute-done((bf16[16,256,128]{2,1,0:T(8,128)(2,1)S(1)}, bf16[16,256,128]{2,1,0:T(8,128)(2,1)S(1)}, u32[]{:S(2)}, u32[]{:S(2)}) %collective-permute-start.12) | collective-permute-done | bytes 1048608 | tf_op jit(solution)/shard_map/ppermute | solution.py:33
  61.0 6.3 %shard_map.72 = f32[1024,512]{1,0:T(8,128)S(1)} custom-call(bf16[1024,4096]{1,0:T(8,128)(2,1)} %shard_map.67.packed, bf16[16,256,128]{2,1,0:T(8,128)(2,1)S(1)} %shard_map.71.left, bf16[16,256,128]{2,1,0:T(8,128)(2,1)S(1)} %collective-permute-done.12.right), custom_call_target="tpu_custom_call" | custom-call | flops 2147483648 | bytes 10485760 | tf_op jit(solution)/shard_map/pallas_call | solution.py:165
  67.3 0.2 fusion.1
  67.5 4.0 %collective-permute-done.10.left = bf16[16,256,128]{2,1,0:T(8,128)(2,1)S(1)} collective-permute-done((bf16[16,256,128]{2,1,0:T(8,128)(2,1)S(1)}, bf16[16,256,128]{2,1,0:T(8,128)(2,1)S(1)}, u32[]{:S(2)}, u32[]{:S(2)}) %collective-permute-start.10) | collective-permute-done | bytes 1048608 | tf_op jit(solution)/shard_map/ppermute | solution.py:33
  71.5 0.7 collective-permute-done.11.right
  72.2 4.8 %shard_map.74 = f32[512,512]{1,0:T(8,128)S(1)} custom-call(bf16[1024,4096]{1,0:T(8,128)(2,1)} %shard_map.67.packed, bf16[16,256,128]{2,1,0:T(8,128)(2,1)S(1)} %collective-permute-done.10.left, bf16[16,256,128]{2,1,0:T(8,128)(2,1)S(1)} %collective-permute-done.11.right, f32[512,512]{1,0:T(8,128)S(1)} %get-tuple-element.20.rest_0_), custom_call_target="tpu_custom_call" | custom-call | flops 1073741824 | bytes 6291456 | tf_op jit(solution)/shard_map/pallas_call | solution.py:165
  77.0 0.1 convert_element_type.9
  77.1 12.8 %collective-permute-start.13 = (bf16[512,512]{1,0:T(8,128)(2,1)S(1)}, bf16[512,512]{1,0:T(8,128)(2,1)S(1)}, u32[]{:S(2)}, u32[]{:S(2)}) collective-permute-start(bf16[512,512]{1,0:T(8,128)(2,1)S(1)} %convert_element_type.9), channel_id=1, source_target_pairs={{0,2},{1,3},{2,0},{3,1},{4,6},{5,7},{6,4},{7,5},{8,10},{9,11},{10,... | collective-permute-start | bytes 1572872 | tf_op jit(solution)/shard_map/ppermute | solution.py:33
  89.9 4.8 %shard_map.73 = f32[512,512]{1,0:T(8,128)S(1)} custom-call(bf16[1024,4096]{1,0:T(8,128)(2,1)} %shard_map.67.packed, bf16[16,256,128]{2,1,0:T(8,128)(2,1)S(1)} %collective-permute-done.10.left, bf16[16,256,128]{2,1,0:T(8,128)(2,1)S(1)} %collective-permute-done.11.right, f32[512,512]{1,0:T(8,128)S(1)} %get-tuple-element.21.rest_0_), custom_call_target="tpu_custom_call" | custom-call | flops 1073741824 | bytes 6291456 | tf_op jit(solution)/shard_map/pallas_call | solution.py:165
  94.7 0.0 collective-permute-done.13
  94.7 1.0 fusion
  (2 shorter events, 0.1 us)
Async XLA Ops:
  0.6 48.1 %collective-permute-start = (bf16[512,8192]{1,0:T(8,128)(2,1)}, bf16[512,8192]{1,0:T(8,128)(2,1)S(1)}, u32[]{:S(2)}, u32[]{:S(2)}) collective-permute-start(bf16[512,8192]{1,0:T(8,128)(2,1)} %bitcast.15), channel_id=1, source_target_pairs={{0,2},{1,3},{2,0},{3,1},{4,6},{5,7},{6,4},{7,5},{8,10},{9,11},{10,... | collective-permute-start | bytes 25165832 | tf_op jit(solution)/shard_map/ppermute | solution.py:33
  4.0 0.9 copy-start
  5.0 5.0 %collective-permute-start.1 = (bf16[256,128]{1,0:T(8,128)(2,1)S(1)}, bf16[256,128]{1,0:T(8,128)(2,1)S(1)}, u32[]{:S(2)}, u32[]{:S(2)}) collective-permute-start(bf16[256,128]{1,0:T(8,128)(2,1)S(1)} %get-tuple-element.11), channel_id=1, source_target_pairs={{0,64},{1,65},{2,66},{3,67},{4,68},{5,69},{6,70},{7,71},{8,72},{9,... | collective-permute-start | bytes 196616 | tf_op jit(solution)/shard_map/ppermute | solution.py:33
  5.1 5.5 %collective-permute-start.2 = (bf16[256,128]{1,0:T(8,128)(2,1)S(1)}, bf16[256,128]{1,0:T(8,128)(2,1)S(1)}, u32[]{:S(2)}, u32[]{:S(2)}) collective-permute-start(bf16[256,128]{1,0:T(8,128)(2,1)S(1)} %get-tuple-element.12), channel_id=1, source_target_pairs={{0,192},{1,193},{2,194},{3,195},{4,196},{5,197},{6,198},{7,199},{8... | collective-permute-start | bytes 196616 | tf_op jit(solution)/shard_map/ppermute | solution.py:33
  7.7 4.6 %collective-permute-start.3 = (bf16[256,128]{1,0:T(8,128)(2,1)S(1)}, bf16[256,128]{1,0:T(8,128)(2,1)S(1)}, u32[]{:S(2)}, u32[]{:S(2)}) collective-permute-start(bf16[256,128]{1,0:T(8,128)(2,1)S(1)} %get-tuple-element.13), channel_id=1, source_target_pairs={{0,128},{1,129},{2,130},{3,131},{4,132},{5,133},{6,134},{7,135},{8... | collective-permute-start | bytes 196616 | tf_op jit(solution)/shard_map/ppermute | solution.py:33
  12.3 0.9 copy-start.1
  13.2 0.9 copy-start.2
  14.9 8.1 %collective-permute-start.4 = (bf16[256,128]{1,0:T(8,128)(2,1)S(1)}, bf16[256,128]{1,0:T(8,128)(2,1)S(1)}, u32[]{:S(2)}, u32[]{:S(2)}) collective-permute-start(bf16[256,128]{1,0:T(8,128)(2,1)S(1)} %get-tuple-element.14.own), channel_id=1, source_target_pairs={{0,32},{1,33},{2,34},{3,35},{4,36},{5,37},{6,38},{7,39},{8,40},{9,... | collective-permute-start | bytes 196616 | tf_op jit(solution)/shard_map/ppermute | solution.py:33
  16.1 8.6 %collective-permute-start.5 = (bf16[256,128]{1,0:T(8,128)(2,1)S(1)}, bf16[256,128]{1,0:T(8,128)(2,1)S(1)}, u32[]{:S(2)}, u32[]{:S(2)}) collective-permute-start(bf16[256,128]{1,0:T(8,128)(2,1)S(1)} %get-tuple-element.14.own), channel_id=1, source_target_pairs={{0,16},{1,17},{2,18},{3,19},{4,20},{5,21},{6,22},{7,23},{8,24},{9,... | collective-permute-start | bytes 196616 | tf_op jit(solution)/shard_map/ppermute | solution.py:33
  23.0 9.4 %collective-permute-start.6 = (bf16[256,128]{1,0:T(8,128)(2,1)S(1)}, bf16[256,128]{1,0:T(8,128)(2,1)S(1)}, u32[]{:S(2)}, u32[]{:S(2)}) collective-permute-start(bf16[256,128]{1,0:T(8,128)(2,1)S(1)} %get-tuple-element.14.own), channel_id=1, source_target_pairs={{0,48},{1,49},{2,50},{3,51},{4,52},{5,53},{6,54},{7,55},{8,56},{9,... | collective-permute-start | bytes 196616 | tf_op jit(solution)/shard_map/ppermute | solution.py:33
  32.5 6.5 %collective-permute-start.7 = (bf16[4,256,128]{2,1,0:T(8,128)(2,1)S(1)}, bf16[4,256,128]{2,1,0:T(8,128)(2,1)S(1)}, u32[]{:S(2)}, u32[]{:S(2)}) collective-permute-start(bf16[4,256,128]{2,1,0:T(8,128)(2,1)S(1)} %shard_map.70.own), channel_id=1, source_target_pairs={{0,64},{1,65},{2,6},{3,7},{4,68},{5,69},{6,10},{7,11},{8,72},{9,73... | collective-permute-start | bytes 786440 | tf_op jit(solution)/shard_map/ppermute | solution.py:33
  33.4 5.6 %collective-permute-start.8 = (bf16[4,256,128]{2,1,0:T(8,128)(2,1)S(1)}, bf16[4,256,128]{2,1,0:T(8,128)(2,1)S(1)}, u32[]{:S(2)}, u32[]{:S(2)}) collective-permute-start(bf16[4,256,128]{2,1,0:T(8,128)(2,1)S(1)} %shard_map.70.own), channel_id=1, source_target_pairs={{0,192},{1,193},{2,30},{3,31},{4,196},{5,197},{6,2},{7,3},{8,200},... | collective-permute-start | bytes 786440 | tf_op jit(solution)/shard_map/ppermute | solution.py:33
  35.2 10.4 %collective-permute-start.9 = (bf16[4,256,128]{2,1,0:T(8,128)(2,1)S(1)}, bf16[4,256,128]{2,1,0:T(8,128)(2,1)S(1)}, u32[]{:S(2)}, u32[]{:S(2)}) collective-permute-start(bf16[4,256,128]{2,1,0:T(8,128)(2,1)S(1)} %shard_map.70.own), channel_id=1, source_target_pairs={{0,128},{1,129},{2,10},{3,11},{4,132},{5,133},{6,14},{7,15},{8,136... | collective-permute-start | bytes 786440 | tf_op jit(solution)/shard_map/ppermute | solution.py:33
  45.8 15.2 %collective-permute-start.12 = (bf16[16,256,128]{2,1,0:T(8,128)(2,1)S(1)}, bf16[16,256,128]{2,1,0:T(8,128)(2,1)S(1)}, u32[]{:S(2)}, u32[]{:S(2)}) collective-permute-start(bf16[16,256,128]{2,1,0:T(8,128)(2,1)S(1)} %shard_map.71.left), channel_id=1, source_target_pairs={{0,4},{1,5},{2,66},{3,67},{4,8},{5,9},{6,70},{7,71},{8,12},{9,13},... | collective-permute-start | bytes 3145736 | tf_op jit(solution)/shard_map/ppermute | solution.py:33
  45.9 25.6 %collective-permute-start.10 = (bf16[16,256,128]{2,1,0:T(8,128)(2,1)S(1)}, bf16[16,256,128]{2,1,0:T(8,128)(2,1)S(1)}, u32[]{:S(2)}, u32[]{:S(2)}) collective-permute-start(bf16[16,256,128]{2,1,0:T(8,128)(2,1)S(1)} %shard_map.71.left), channel_id=1, source_target_pairs={{0,28},{1,29},{2,194},{3,195},{4,0},{5,1},{6,198},{7,199},{8,4},{9... | collective-permute-start | bytes 3145736 | tf_op jit(solution)/shard_map/ppermute | solution.py:33
  48.5 23.7 %collective-permute-start.11 = (bf16[16,256,128]{2,1,0:T(8,128)(2,1)S(1)}, bf16[16,256,128]{2,1,0:T(8,128)(2,1)S(1)}, u32[]{:S(2)}, u32[]{:S(2)}) collective-permute-start(bf16[16,256,128]{2,1,0:T(8,128)(2,1)S(1)} %shard_map.71.left), channel_id=1, source_target_pairs={{0,8},{1,9},{2,130},{3,131},{4,12},{5,13},{6,134},{7,135},{8,16},{... | collective-permute-start | bytes 3145736 | tf_op jit(solution)/shard_map/ppermute | solution.py:33
  48.7 3.2 %copy-start.3 = (bf16[512,8192]{1,0:T(8,128)(2,1)}, bf16[512,8192]{1,0:T(8,128)(2,1)S(1)}, u32[]{:S(2)}) copy-start(bf16[512,8192]{1,0:T(8,128)(2,1)S(1)} %collective-permute-done.other) | copy-start | bytes 25165828
  77.1 17.7 %collective-permute-start.13 = (bf16[512,512]{1,0:T(8,128)(2,1)S(1)}, bf16[512,512]{1,0:T(8,128)(2,1)S(1)}, u32[]{:S(2)}, u32[]{:S(2)}) collective-permute-start(bf16[512,512]{1,0:T(8,128)(2,1)S(1)} %convert_element_type.9), channel_id=1, source_target_pairs={{0,2},{1,3},{2,0},{3,1},{4,6},{5,7},{6,4},{7,5},{8,10},{9,11},{10,... | collective-permute-start | bytes 1572872 | tf_op jit(solution)/shard_map/ppermute | solution.py:33

commit v2 on v1

v2 whole, which is shorter than its diff:
```python
import functools

import jax
import jax.numpy as jnp
from jax import lax
from jax.experimental import pallas as pl
from jax.experimental.pallas import tpu as pltpu
from jax.sharding import PartitionSpec as P

outer_rate = 0.7
momentum_keep = 0.9

AXES = ("replica", "fsdp", "tensor")
STEPS = (1, -1, 2)
VMEM_LIMIT = 20 * 1024 * 1024


def pairs(move):
    out = []
    for x in range(4):
        for y in range(2):
            for z in range(8):
                for c in range(2):
                    for t in range(2):
                        to_x, to_y, to_z, to_c = move(x, y, z, c)
                        source = (x * 32 + y * 16 + z * 2 + c) * 2 + t
                        target = ((to_x % 4) * 32 + (to_y % 2) * 16 + (to_z % 8) * 2 + to_c % 2) * 2 + t
                        out.append((source, target))
    return out


def send(value, move):
    return lax.ppermute(value, AXES, pairs(move))


def along_x(step):
    return lambda x, y, z, c: (x + step, y, z, c)


def early(step):
    def move(x, y, z, c):
        along_z = step if step != 2 or z % 2 == 0 else -step
        return (x + step, y, z, c) if c == 0 else (x, y, z + along_z, c)

    return move


def late(step):
    return lambda x, y, z, c: (x, y, z + step, c) if c == 0 else (x + step, y, z, c)


def position():
    index = lax.axis_index("fsdp")
    return lax.axis_index("replica"), index // 16, (index // 2) % 8, index % 2


def wrap(value):
    return lax.rem(value + 4, 4)


def call(kernel, out_shape, *, flops=0, size=1, scratch=(), in_specs=None):
    specs = {} if in_specs is None else {"in_specs": in_specs}
    return pl.pallas_call(
        kernel,
        out_shape=out_shape,
        **specs,
        scratch_shapes=list(scratch),
        compiler_params=pltpu.CompilerParams(vmem_limit_bytes=VMEM_LIMIT),
        cost_estimate=pl.CostEstimate(flops=flops, bytes_accessed=size, transcendentals=0),
    )


def split_kernel(grad, *outs):
    x, _, _, _ = position()
    for step, out in zip((0,) + STEPS, outs):
        first = pl.multiple_of(wrap(x + step) * 128, 128)
        out[...] = grad[:, pl.ds(first, 128)]


def prepare_kernel(anchor, momentum, anchor_out, kept_out):
    anchor_out[...] = anchor[...]
    kept_out[...] = momentum_keep * momentum[...]


def step_of(own, one, two, three, anchor, kept):
    total = own[...].astype(jnp.float32) + one[...].astype(jnp.float32)
    total = total + (two[...].astype(jnp.float32) + three[...].astype(jnp.float32))
    delta = total * 0.25
    momentum_new = kept[...] + delta
    return anchor[...] - outer_rate * (delta + momentum_keep * momentum_new), momentum_new


def weights_kernel(own, one, two, three, anchor, kept, weights):
    weights[...] = step_of(own, one, two, three, anchor, kept)[0].astype(jnp.bfloat16)


def state_kernel(own, one, two, three, anchor, kept, anchor_new, momentum_new):
    anchor_new[...], momentum_new[...] = step_of(own, one, two, three, anchor, kept)


def join_y_kernel(own, other, out):
    _, y, _, _ = position()
    out[y] = own[...]
    out[1 - y] = other[...]


def join_far_kernel(own, other, out):
    _, _, z, _ = position()
    far = z // 4
    out[pl.ds(far * 2, 2)] = own[...]
    out[pl.ds((1 - far) * 2, 2)] = other[...]


def join_four_kernel(own, one, two, three, low, high):
    x, _, z, c = position()
    here = jnp.where(c == 0, x, z % 4)
    for step, piece in zip((0,) + STEPS, (own, one, two, three)):
        place = wrap(here - step)
        row = lax.rem(place, 2) * 4

        @pl.when(place < 2)
        def _():
            low[pl.ds(row, 4)] = piece[...]

        @pl.when(place >= 2)
        def _():
            high[pl.ds(row, 4)] = piece[...]


def pack_kernel(own, other, out, sems):
    _, _, _, c = position()
    copies = []
    for side, tokens in enumerate((own, other)):
        for near in range(4):
            for pair in range(4):
                row = (pair % 2) * 16 + ((pair // 2) * 4 + near) * 2
                source = pl.multiple_of((row + c) * 256, 256)
                copies.append(
                    pltpu.make_async_copy(
                        tokens.at[:, pl.ds(source, 256)],
                        out.at[pl.ds(side * 512, 512), pl.ds((near * 4 + pair) * 256, 256)],
                        sems.at[len(copies)],
                    )
                )
    for copy in copies:
        copy.start()
    for copy in copies:
        copy.wait()


def product_kernel(steps, sides, has_start, packed, *refs):
    count = len(steps)
    lows, highs = refs[:count], refs[count : 2 * count]
    starts = refs[2 * count : 2 * count + len(sides)] if has_start else (None,) * len(sides)
    outs = refs[len(refs) - len(sides) :]
    x, _, z, c = position()

    @pl.when(c == 0)
    def _():
        for side, start, out in zip(sides, starts, outs):
            rows = pl.ds(side * 512, 512)
            for half, pieces in enumerate((lows, highs)):
                columns = pl.ds(half * 256, 256)
                total = start[:, columns] if has_start else None
                for step, piece in zip(steps, pieces):
                    near = pl.multiple_of(wrap(z % 4 - step) * 1024, 1024)
                    block = jnp.concatenate([piece[pl.ds(q * 4, 4)].reshape(1024, 128) for q in range(2)], axis=1)
                    term = jnp.dot(packed[rows, pl.ds(near, 1024)], block, preferred_element_type=jnp.float32)
                    total = term if total is None else total + term
                out[:, columns] = total.astype(out.dtype)

    @pl.when(c == 1)
    def _():
        for side, start, out in zip(sides, starts, outs):
            rows = pl.ds(side * 512, 512)
            total = None
            for half, pieces in enumerate((lows, highs)):
                block = jnp.concatenate([piece[...].reshape(2048, 128) for piece in pieces], axis=1)
                term = jnp.dot(packed[rows, pl.ds(half * 2048, 2048)], block, preferred_element_type=jnp.float32)
                total = term if total is None else total + term
            if has_start:
                out[...] = start[...].astype(out.dtype)
            for k, step in enumerate(steps):
                column = pl.multiple_of(wrap(x - step) * 128, 128)
                out[:, pl.ds(column, 128)] = total[:, k * 128 : (k + 1) * 128].astype(out.dtype)


def product(packed, steps, lows, highs, sides, starts=(), dtype=jnp.float32):
    count = len(steps) * len(sides)
    return call(
        functools.partial(product_kernel, steps, sides, bool(starts)),
        (jax.ShapeDtypeStruct((512, 512), dtype),) * len(sides),
        flops=2 * count * 512 * 1024 * 512,
        size=count * 2**20,
    )(packed, *lows, *highs, *starts)


def per_device(tokens, pseudo_grad, anchor, momentum):
    def blocks(count):
        return jax.ShapeDtypeStruct((count, 256, 128), jnp.bfloat16)

    block = jax.ShapeDtypeStruct((256, 128), jnp.bfloat16)
    state = jax.ShapeDtypeStruct((256, 128), jnp.float32)
    own_tokens = tokens[0]
    grads = call(split_kernel, (block,) * 4, size=2**19)(pseudo_grad[0])
    arrived = [send(grads[k + 1], along_x(step)) for k, step in enumerate(STEPS)]
    other_tokens = send(own_tokens, lambda x, y, z, c: (x, y, z, c + 1))
    prepared = call(prepare_kernel, (state, state), size=2**19)(anchor.reshape(256, 128), momentum.reshape(256, 128))
    (weights,) = call(weights_kernel, (block,), size=2**19)(grads[0], *arrived, *prepared)
    anchor_new, momentum_new = call(state_kernel, (state, state), size=2**20)(grads[0], *arrived, *prepared)
    by_y = send(weights, lambda x, y, z, c: (x, y + 1, z, c))
    (two,) = call(join_y_kernel, (blocks(2),), size=2**18)(weights, by_y)
    by_far = send(two, lambda x, y, z, c: (x, y, z + 4, c))
    (four,) = call(join_far_kernel, (blocks(4),), size=2**19)(two, by_far)
    fours = [send(four, early(step)) for step in STEPS]
    low, high = call(join_four_kernel, (blocks(8), blocks(8)), size=2**21)(four, *fours)
    (packed,) = call(
        pack_kernel,
        (jax.ShapeDtypeStruct((1024, 4096), jnp.bfloat16),),
        size=2**24,
        scratch=(pltpu.SemaphoreType.DMA((32,)),),
        in_specs=[pl.BlockSpec(memory_space=pl.ANY), pl.BlockSpec(memory_space=pltpu.VMEM)],
    )(own_tokens, other_tokens)
    low_up, high_down = send(low, late(1)), send(high, late(-1))
    high_up, low_down = send(high, late(1)), send(low, late(-1))
    low_two, high_two = send(low_up, late(1)), send(high_down, late(-1))
    starts = product(packed, (0,), (low,), (high,), (0, 1))
    starts = product(packed, (1, -1), (low_up, low_down), (high_up, high_down), (0, 1), starts)
    (away,) = product(packed, (2,), (low_two,), (high_two,), (1,), starts[1:], jnp.bfloat16)
    returned = send(away, lambda x, y, z, c: (x, y, z, c + 1))
    (here,) = product(packed, (2,), (low_two,), (high_two,), (0,), starts[:1])
    keys = (here + returned.astype(jnp.float32)).astype(jnp.bfloat16)[None]
    return keys, anchor_new.reshape(anchor.shape), momentum_new.reshape(momentum.shape)


def solution(mesh):
    return jax.shard_map(
        per_device,
        mesh=mesh,
        in_specs=(
            P("replica", "fsdp", None),
            P("replica", "fsdp", "tensor"),
            P("fsdp", "tensor", "replica", None),
            P("fsdp", "tensor", "replica", None),
        ),
        out_specs=(
            P("replica", "fsdp", "tensor"),
            P("fsdp", "tensor", "replica", None),
            P("fsdp", "tensor", "replica", None),
        ),
        check_vma=False,
    )
```

time: 96 us -> 71.4 us (0.74)
  the two profiles are of different devices: /device:TPU:1 before, /device:TPU:113 now
where the time goes in v2:
time: 71.4 us; the launch traced here: 71.2 us
  starting transfers between devices  29.6 us (41%)
  waiting for transfers between devices  23.9 us (33%)
  Pallas kernels  9.83 us (14%)
  local copies, waits for them, and re-layouts  6.14 us (9%)
  other arithmetic  0.95 us (1%)
  between operations  0.77 us (1%)
    ppermute x16, starting transfers between devices, send(): return lax.ppermute(value, AXES, pairs(move))  29.6 us
    ppermute x16, waiting for transfers between devices, send(): return lax.ppermute(value, AXES, pairs(move))  23.9 us
    pallas_call x4, Pallas kernels, product(): call(functools.partial(product_kernel, steps, sides, bool(starts)), (jax....  7.2 us
    unnamed x8, local copies, waits for them, and re-layouts  6.14 us
    pallas_call x1, Pallas kernels, per_device(): call(pack_kernel, (jax.ShapeDtypeStruct((1024, 4096), jnp.bfloat16),), si...  1.6 us
  transfers between devices with their start and end apart: 16, of which 7 were waited for; matrix products, arithmetic and copies ran while one was open for 0% of the time, Pallas kernels for 12%

profile of v2, /device:TPU:113, one launch (start us, length us, event | category | flops | bytes accessed | tf_op | source)
XLA Modules:
  0.0 71.2 jit_solution(11042970539655387801)
XLA Ops:
  0.6 0.8 %collective-permute-start = (bf16[512,8192]{1,0:T(8,128)(2,1)}, bf16[512,8192]{1,0:T(8,128)(2,1)S(1)}, u32[]{:S(2)}, u32[]{:S(2)}) collective-permute-start(bf16[512,8192]{1,0:T(8,128)(2,1)} %bitcast.12), channel_id=1, source_target_pairs={{0,2},{1,3},{2,0},{3,1},{4,6},{5,7},{6,4},{7,5},{8,10},{9,11},{10,... | collective-permute-start | bytes 25165832 | tf_op jit(solution)/shard_map/ppermute | solution.py:33
  1.4 0.0 copy-start.1
  1.4 0.9 %copy-done.1 = bf16[1,256,512]{2,1,0:T(8,128)(2,1)S(1)} copy-done((bf16[1,256,512]{2,1,0:T(8,128)(2,1)S(1)}, bf16[1,256,512]{2,1,0:T(8,128)(2,1)}, u32[]{:S(2)}) %copy-start.1) | copy-done | bytes 262168
  2.4 1.3 %collective-permute-start.1 = (bf16[256,128]{1,0:T(8,128)(2,1)S(1)}, bf16[256,128]{1,0:T(8,128)(2,1)S(1)}, u32[]{:S(2)}, u32[]{:S(2)}) collective-permute-start(bf16[256,128]{1,0:T(8,128)(2,1)S(1)} %get-tuple-element.18), channel_id=1, source_target_pairs={{0,64},{1,65},{2,66},{3,67},{4,68},{5,69},{6,70},{7,71},{8,72},{9,... | collective-permute-start | bytes 196616 | tf_op jit(solution)/shard_map/ppermute | solution.py:33
  3.7 1.5 %collective-permute-start.2 = (bf16[256,128]{1,0:T(8,128)(2,1)S(1)}, bf16[256,128]{1,0:T(8,128)(2,1)S(1)}, u32[]{:S(2)}, u32[]{:S(2)}) collective-permute-start(bf16[256,128]{1,0:T(8,128)(2,1)S(1)} %get-tuple-element.19), channel_id=1, source_target_pairs={{0,192},{1,193},{2,194},{3,195},{4,196},{5,197},{6,198},{7,199},{8... | collective-permute-start | bytes 196616 | tf_op jit(solution)/shard_map/ppermute | solution.py:33
  5.1 1.5 %collective-permute-start.3 = (bf16[256,128]{1,0:T(8,128)(2,1)S(1)}, bf16[256,128]{1,0:T(8,128)(2,1)S(1)}, u32[]{:S(2)}, u32[]{:S(2)}) collective-permute-start(bf16[256,128]{1,0:T(8,128)(2,1)S(1)} %get-tuple-element.20), channel_id=1, source_target_pairs={{0,128},{1,129},{2,130},{3,131},{4,132},{5,133},{6,134},{7,135},{8... | collective-permute-start | bytes 196616 | tf_op jit(solution)/shard_map/ppermute | solution.py:33
  6.7 0.0 copy-start.2
  6.7 0.9 %copy-done.2 = f32[256,1,1,128]{3,2,1,0:T(1,128)S(1)} copy-done((f32[256,1,1,128]{3,2,1,0:T(1,128)S(1)}, f32[256,1,1,128]{3,2,1,0:T(1,128)}, u32[]{:S(2)}) %copy-start.2) | copy-done | bytes 131096
  7.6 0.0 copy-start.3
  7.6 0.9 %copy-done.3 = f32[256,1,1,128]{3,2,1,0:T(1,128)S(1)} copy-done((f32[256,1,1,128]{3,2,1,0:T(1,128)S(1)}, f32[256,1,1,128]{3,2,1,0:T(1,128)}, u32[]{:S(2)}) %copy-start.3) | copy-done | bytes 131096
  8.5 0.0 collective-permute-done.1.one
  8.5 0.0 collective-permute-done.2.two
  8.5 1.2 %collective-permute-done.3.three = bf16[256,128]{1,0:T(8,128)(2,1)S(1)} collective-permute-done((bf16[256,128]{1,0:T(8,128)(2,1)S(1)}, bf16[256,128]{1,0:T(8,128)(2,1)S(1)}, u32[]{:S(2)}, u32[]{:S(2)}) %collective-permute-start.3) | collective-permute-done | bytes 65568 | tf_op jit(solution)/shard_map/ppermute | solution.py:33
  9.8 0.1 shard_map.70.own
  9.8 0.1 collective-permute-start.4
  10.0 4.6 %collective-permute-done.4.other = bf16[256,128]{1,0:T(8,128)(2,1)S(1)} collective-permute-done((bf16[256,128]{1,0:T(8,128)(2,1)S(1)}, bf16[256,128]{1,0:T(8,128)(2,1)S(1)}, u32[]{:S(2)}, u32[]{:S(2)}) %collective-permute-start.4) | collective-permute-done | bytes 65568 | tf_op jit(solution)/shard_map/ppermute | solution.py:33
  14.6 4.3 %collective-permute-start.5 = (bf16[2,256,128]{2,1,0:T(8,128)(2,1)S(1)}, bf16[2,256,128]{2,1,0:T(8,128)(2,1)S(1)}, u32[]{:S(2)}, u32[]{:S(2)}) collective-permute-start(bf16[2,256,128]{2,1,0:T(8,128)(2,1)S(1)} %shard_map.71.own), channel_id=1, source_target_pairs={{0,16},{1,17},{2,18},{3,19},{4,20},{5,21},{6,22},{7,23},{8,24},{9,... | collective-permute-start | bytes 393224 | tf_op jit(solution)/shard_map/ppermute | solution.py:33
  18.9 3.6 %collective-permute-done.5.other = bf16[2,256,128]{2,1,0:T(8,128)(2,1)S(1)} collective-permute-done((bf16[2,256,128]{2,1,0:T(8,128)(2,1)S(1)}, bf16[2,256,128]{2,1,0:T(8,128)(2,1)S(1)}, u32[]{:S(2)}, u32[]{:S(2)}) %collective-permute-start.5) | collective-permute-done | bytes 131104 | tf_op jit(solution)/shard_map/ppermute | solution.py:33
  22.5 3.6 %collective-permute-start.6 = (bf16[4,256,128]{2,1,0:T(8,128)(2,1)S(1)}, bf16[4,256,128]{2,1,0:T(8,128)(2,1)S(1)}, u32[]{:S(2)}, u32[]{:S(2)}) collective-permute-start(bf16[4,256,128]{2,1,0:T(8,128)(2,1)S(1)} %shard_map.72.own), channel_id=1, source_target_pairs={{0,64},{1,65},{2,6},{3,7},{4,68},{5,69},{6,10},{7,11},{8,72},{9,73... | collective-permute-start | bytes 786440 | tf_op jit(solution)/shard_map/ppermute | solution.py:33
  26.1 0.0 collective-permute-start.7
  26.1 0.0 collective-permute-start.8
  26.1 3.9 %collective-permute-done.6.one = bf16[4,256,128]{2,1,0:T(8,128)(2,1)S(1)} collective-permute-done((bf16[4,256,128]{2,1,0:T(8,128)(2,1)S(1)}, bf16[4,256,128]{2,1,0:T(8,128)(2,1)S(1)}, u32[]{:S(2)}, u32[]{:S(2)}) %collective-permute-start.6) | collective-permute-done | bytes 262176 | tf_op jit(solution)/shard_map/ppermute | solution.py:33
  30.0 2.8 %collective-permute-done.7.two = bf16[4,256,128]{2,1,0:T(8,128)(2,1)S(1)} collective-permute-done((bf16[4,256,128]{2,1,0:T(8,128)(2,1)S(1)}, bf16[4,256,128]{2,1,0:T(8,128)(2,1)S(1)}, u32[]{:S(2)}, u32[]{:S(2)}) %collective-permute-start.7) | collective-permute-done | bytes 262176 | tf_op jit(solution)/shard_map/ppermute | solution.py:33
  32.8 2.7 %collective-permute-done.8.three = bf16[4,256,128]{2,1,0:T(8,128)(2,1)S(1)} collective-permute-done((bf16[4,256,128]{2,1,0:T(8,128)(2,1)S(1)}, bf16[4,256,128]{2,1,0:T(8,128)(2,1)S(1)}, u32[]{:S(2)}, u32[]{:S(2)}) %collective-permute-start.8) | collective-permute-done | bytes 262176 | tf_op jit(solution)/shard_map/ppermute | solution.py:33
  35.5 0.1 shard_map.73
  35.7 0.2 collective-permute-start.9
  35.8 2.6 %collective-permute-start.11 = (bf16[8,256,128]{2,1,0:T(8,128)(2,1)S(1)}, bf16[8,256,128]{2,1,0:T(8,128)(2,1)S(1)}, u32[]{:S(2)}, u32[]{:S(2)}) collective-permute-start(bf16[8,256,128]{2,1,0:T(8,128)(2,1)S(1)} %get-tuple-element.24.refs_1_), channel_id=1, source_target_pairs={{0,28},{1,29},{2,194},{3,195},{4,0},{5,1},{6,198},{7,199},{8,4},{9... | collective-permute-start | bytes 1572872 | tf_op jit(solution)/shard_map/ppermute | solution.py:33
  38.4 0.1 collective-permute-start.13
  38.5 1.4 %collective-permute-start.14 = (bf16[8,256,128]{2,1,0:T(8,128)(2,1)S(1)}, bf16[8,256,128]{2,1,0:T(8,128)(2,1)S(1)}, u32[]{:S(2)}, u32[]{:S(2)}) collective-permute-start(bf16[8,256,128]{2,1,0:T(8,128)(2,1)S(1)} %get-tuple-element.24.refs_1_), channel_id=1, source_target_pairs={{0,4},{1,5},{2,66},{3,67},{4,8},{5,9},{6,70},{7,71},{8,12},{9,13},... | collective-permute-start | bytes 1572872 | tf_op jit(solution)/shard_map/ppermute | solution.py:33
  39.9 5.1 %collective-permute-done.9.refs_0_ = bf16[8,256,128]{2,1,0:T(8,128)(2,1)S(1)} collective-permute-done((bf16[8,256,128]{2,1,0:T(8,128)(2,1)S(1)}, bf16[8,256,128]{2,1,0:T(8,128)(2,1)S(1)}, u32[]{:S(2)}, u32[]{:S(2)}) %collective-permute-start.9) | collective-permute-done | bytes 524320 | tf_op jit(solution)/shard_map/ppermute | solution.py:33
  45.0 0.0 collective-permute-start.10
  45.0 0.0 collective-permute-done.11.refs_3_
  45.0 2.7 %collective-permute-start.12 = (bf16[8,256,128]{2,1,0:T(8,128)(2,1)S(1)}, bf16[8,256,128]{2,1,0:T(8,128)(2,1)S(1)}, u32[]{:S(2)}, u32[]{:S(2)}) collective-permute-start(bf16[8,256,128]{2,1,0:T(8,128)(2,1)S(1)} %collective-permute-done.11.refs_3_), channel_id=1, source_target_pairs={{0,28},{1,29},{2,194},{3,195},{4,0},{5,1},{6,198},{7,199},{8,4},{9... | collective-permute-start | bytes 1572872 | tf_op jit(solution)/shard_map/ppermute | solution.py:33
  47.7 0.0 collective-permute-done.other
  47.7 0.0 copy-start
  47.7 3.4 %copy-done = bf16[1,512,8192]{2,1,0:T(8,128)(2,1)S(1)} copy-done((bf16[1,512,8192]{2,1,0:T(8,128)(2,1)S(1)}, bf16[1,512,8192]{2,1,0:T(8,128)(2,1)}, u32[]{:S(2)}) %copy-start) | copy-done | bytes 8388632
  51.0 1.6 %shard_map.67.packed = bf16[1024,4096]{1,0:T(8,128)(2,1)S(1)} custom-call(bf16[512,8192]{1,0:T(8,128)(2,1)S(1)} %bitcast.13, bf16[512,8192]{1,0:T(8,128)(2,1)S(1)} %collective-permute-done.other), custom_call_target="tpu_custom_call" | custom-call | bytes 16777216 | tf_op jit(solution)/shard_map/pallas_call | solution.py:217
  52.6 2.3 %shard_map.74 = (f32[512,512]{1,0:T(8,128)S(1)}, f32[512,512]{1,0:T(8,128)S(1)}) custom-call(bf16[1024,4096]{1,0:T(8,128)(2,1)S(1)} %shard_map.67.packed, bf16[8,256,128]{2,1,0:T(8,128)(2,1)S(1)} %get-tuple-element.23.refs_0_, bf16[8,256,128]{2,1,0:T(8,128)(2,1)S(1)} %get-tuple-element.24.refs_1_), custom_call_target="tpu_custom_call" | custom-call | flops 1073741824 | bytes 2097152 | tf_op jit(solution)/shard_map/pallas_call | solution.py:190
  55.0 0.0 collective-permute-done.13.refs_1_
  55.0 0.0 collective-permute-done.14.refs_2_
  55.0 2.3 %shard_map.75 = (f32[512,512]{1,0:T(8,128)S(1)}, f32[512,512]{1,0:T(8,128)S(1)}) custom-call(bf16[1024,4096]{1,0:T(8,128)(2,1)S(1)} %shard_map.67.packed, bf16[8,256,128]{2,1,0:T(8,128)(2,1)S(1)} %collective-permute-done.9.refs_0_, bf16[8,256,128]{2,1,0:T(8,128)(2,1)S(1)} %collective-permute-done.13.refs_1_, ...), custom_call_target="tpu_custom_call" | custom-call | flops 2147483648 | bytes 4194304 | tf_op jit(solution)/shard_map/pallas_call | solution.py:190
  57.4 0.0 collective-permute-done.10.refs_0_
  57.4 0.0 collective-permute-done.12.refs_1_
  57.4 1.3 %shard_map.77 = bf16[512,512]{1,0:T(8,128)(2,1)S(1)} custom-call(bf16[1024,4096]{1,0:T(8,128)(2,1)S(1)} %shard_map.67.packed, bf16[8,256,128]{2,1,0:T(8,128)(2,1)S(1)} %collective-permute-done.10.refs_0_, bf16[8,256,128]{2,1,0:T(8,128)(2,1)S(1)} %collective-permute-done.12.refs_1_, f32[512,512]{1,0:T(8,128)S(1)} %get-tuple-element.28.refs_2_), custom_call_target="tpu_custom_call" | custom-call | flops 536870912 | bytes 1048576 | tf_op jit(solution)/shard_map/pallas_call | solution.py:190
  58.7 9.6 %collective-permute-start.15 = (bf16[512,512]{1,0:T(8,128)(2,1)S(1)}, bf16[512,512]{1,0:T(8,128)(2,1)S(1)}, u32[]{:S(2)}, u32[]{:S(2)}) collective-permute-start(bf16[512,512]{1,0:T(8,128)(2,1)S(1)} %shard_map.77), channel_id=1, source_target_pairs={{0,2},{1,3},{2,0},{3,1},{4,6},{5,7},{6,4},{7,5},{8,10},{9,11},{10,... | collective-permute-start | bytes 1572872 | tf_op jit(solution)/shard_map/ppermute | solution.py:33
  68.2 0.8 %shard_map.78 = (f32[256,128]{1,0:T(8,128)}, f32[256,128]{1,0:T(8,128)}) custom-call(bf16[256,128]{1,0:T(8,128)(2,1)S(1)} %get-tuple-element.17.own, bf16[256,128]{1,0:T(8,128)(2,1)S(1)} %collective-permute-done.1.one, bf16[256,128]{1,0:T(8,128)(2,1)S(1)} %collective-permute-done.2.two, bf16[256,128]{1,0:T(8,128)(2,1)S(1)} %collective-permute-done.3.three, ...), custom_call_target="tpu_custom_call" | custom-call | bytes 1048576 | tf_op jit(solution)/shard_map/pallas_call | solution.py:210
  69.0 1.2 %shard_map.76 = f32[512,512]{1,0:T(8,128)S(1)} custom-call(bf16[1024,4096]{1,0:T(8,128)(2,1)S(1)} %shard_map.67.packed, bf16[8,256,128]{2,1,0:T(8,128)(2,1)S(1)} %collective-permute-done.10.refs_0_, bf16[8,256,128]{2,1,0:T(8,128)(2,1)S(1)} %collective-permute-done.12.refs_1_, f32[512,512]{1,0:T(8,128)S(1)} %get-tuple-element.27.refs_2_), custom_call_target="tpu_custom_call" | custom-call | flops 536870912 | bytes 1048576 | tf_op jit(solution)/shard_map/pallas_call | solution.py:190
  70.2 0.0 collective-permute-done.15
  70.3 1.0 %fusion = bf16[1,512,512]{2,1,0:T(8,128)(2,1)} fusion(f32[512,512]{1,0:T(8,128)S(1)} %shard_map.76, bf16[512,512]{1,0:T(8,128)(2,1)S(1)} %collective-permute-done.15), kind=kLoop, calls=%fused_computation.1 | loop fusion | flops 786432 | bytes 2097152 | tf_op jit(solution)/shard_map/broadcast_in_dim | solution.py:232
  (4 shorter events, 0.1 us)
Async XLA Ops:
  0.6 47.0 %collective-permute-start = (bf16[512,8192]{1,0:T(8,128)(2,1)}, bf16[512,8192]{1,0:T(8,128)(2,1)S(1)}, u32[]{:S(2)}, u32[]{:S(2)}) collective-permute-start(bf16[512,8192]{1,0:T(8,128)(2,1)} %bitcast.12), channel_id=1, source_target_pairs={{0,2},{1,3},{2,0},{3,1},{4,6},{5,7},{6,4},{7,5},{8,10},{9,11},{10,... | collective-permute-start | bytes 25165832 | tf_op jit(solution)/shard_map/ppermute | solution.py:33
  1.4 0.9 %copy-start.1 = (bf16[1,256,512]{2,1,0:T(8,128)(2,1)S(1)}, bf16[1,256,512]{2,1,0:T(8,128)(2,1)}, u32[]{:S(2)}) copy-start(bf16[1,256,512]{2,1,0:T(8,128)(2,1)} %param.5) | copy-start | bytes 786436
  2.4 6.1 %collective-permute-start.1 = (bf16[256,128]{1,0:T(8,128)(2,1)S(1)}, bf16[256,128]{1,0:T(8,128)(2,1)S(1)}, u32[]{:S(2)}, u32[]{:S(2)}) collective-permute-start(bf16[256,128]{1,0:T(8,128)(2,1)S(1)} %get-tuple-element.18), channel_id=1, source_target_pairs={{0,64},{1,65},{2,66},{3,67},{4,68},{5,69},{6,70},{7,71},{8,72},{9,... | collective-permute-start | bytes 196616 | tf_op jit(solution)/shard_map/ppermute | solution.py:33
  3.7 4.8 %collective-permute-start.2 = (bf16[256,128]{1,0:T(8,128)(2,1)S(1)}, bf16[256,128]{1,0:T(8,128)(2,1)S(1)}, u32[]{:S(2)}, u32[]{:S(2)}) collective-permute-start(bf16[256,128]{1,0:T(8,128)(2,1)S(1)} %get-tuple-element.19), channel_id=1, source_target_pairs={{0,192},{1,193},{2,194},{3,195},{4,196},{5,197},{6,198},{7,199},{8... | collective-permute-start | bytes 196616 | tf_op jit(solution)/shard_map/ppermute | solution.py:33
  5.1 4.6 %collective-permute-start.3 = (bf16[256,128]{1,0:T(8,128)(2,1)S(1)}, bf16[256,128]{1,0:T(8,128)(2,1)S(1)}, u32[]{:S(2)}, u32[]{:S(2)}) collective-permute-start(bf16[256,128]{1,0:T(8,128)(2,1)S(1)} %get-tuple-element.20), channel_id=1, source_target_pairs={{0,128},{1,129},{2,130},{3,131},{4,132},{5,133},{6,134},{7,135},{8... | collective-permute-start | bytes 196616 | tf_op jit(solution)/shard_map/ppermute | solution.py:33
  6.7 0.9 %copy-start.2 = (f32[256,1,1,128]{3,2,1,0:T(1,128)S(1)}, f32[256,1,1,128]{3,2,1,0:T(1,128)}, u32[]{:S(2)}) copy-start(f32[256,1,1,128]{3,2,1,0:T(1,128)} %param.6) | copy-start | bytes 393220
  7.6 0.9 %copy-start.3 = (f32[256,1,1,128]{3,2,1,0:T(1,128)S(1)}, f32[256,1,1,128]{3,2,1,0:T(1,128)}, u32[]{:S(2)}) copy-start(f32[256,1,1,128]{3,2,1,0:T(1,128)} %param.7) | copy-start | bytes 393220
  9.8 4.7 %collective-permute-start.4 = (bf16[256,128]{1,0:T(8,128)(2,1)S(1)}, bf16[256,128]{1,0:T(8,128)(2,1)S(1)}, u32[]{:S(2)}, u32[]{:S(2)}) collective-permute-start(bf16[256,128]{1,0:T(8,128)(2,1)S(1)} %shard_map.70.own), channel_id=1, source_target_pairs={{0,32},{1,33},{2,34},{3,35},{4,36},{5,37},{6,38},{7,39},{8,40},{9,... | collective-permute-start | bytes 196616 | tf_op jit(solution)/shard_map/ppermute | solution.py:33
  14.6 7.9 %collective-permute-start.5 = (bf16[2,256,128]{2,1,0:T(8,128)(2,1)S(1)}, bf16[2,256,128]{2,1,0:T(8,128)(2,1)S(1)}, u32[]{:S(2)}, u32[]{:S(2)}) collective-permute-start(bf16[2,256,128]{2,1,0:T(8,128)(2,1)S(1)} %shard_map.71.own), channel_id=1, source_target_pairs={{0,16},{1,17},{2,18},{3,19},{4,20},{5,21},{6,22},{7,23},{8,24},{9,... | collective-permute-start | bytes 393224 | tf_op jit(solution)/shard_map/ppermute | solution.py:33
  22.5 7.5 %collective-permute-start.6 = (bf16[4,256,128]{2,1,0:T(8,128)(2,1)S(1)}, bf16[4,256,128]{2,1,0:T(8,128)(2,1)S(1)}, u32[]{:S(2)}, u32[]{:S(2)}) collective-permute-start(bf16[4,256,128]{2,1,0:T(8,128)(2,1)S(1)} %shard_map.72.own), channel_id=1, source_target_pairs={{0,64},{1,65},{2,6},{3,7},{4,68},{5,69},{6,10},{7,11},{8,72},{9,73... | collective-permute-start | bytes 786440 | tf_op jit(solution)/shard_map/ppermute | solution.py:33
  26.1 6.7 %collective-permute-start.7 = (bf16[4,256,128]{2,1,0:T(8,128)(2,1)S(1)}, bf16[4,256,128]{2,1,0:T(8,128)(2,1)S(1)}, u32[]{:S(2)}, u32[]{:S(2)}) collective-permute-start(bf16[4,256,128]{2,1,0:T(8,128)(2,1)S(1)} %shard_map.72.own), channel_id=1, source_target_pairs={{0,192},{1,193},{2,30},{3,31},{4,196},{5,197},{6,2},{7,3},{8,200},... | collective-permute-start | bytes 786440 | tf_op jit(solution)/shard_map/ppermute | solution.py:33
  26.1 9.5 %collective-permute-start.8 = (bf16[4,256,128]{2,1,0:T(8,128)(2,1)S(1)}, bf16[4,256,128]{2,1,0:T(8,128)(2,1)S(1)}, u32[]{:S(2)}, u32[]{:S(2)}) collective-permute-start(bf16[4,256,128]{2,1,0:T(8,128)(2,1)S(1)} %shard_map.72.own), channel_id=1, source_target_pairs={{0,128},{1,129},{2,10},{3,11},{4,132},{5,133},{6,30},{7,31},{8,136... | collective-permute-start | bytes 786440 | tf_op jit(solution)/shard_map/ppermute | solution.py:33
  35.7 9.3 %collective-permute-start.9 = (bf16[8,256,128]{2,1,0:T(8,128)(2,1)S(1)}, bf16[8,256,128]{2,1,0:T(8,128)(2,1)S(1)}, u32[]{:S(2)}, u32[]{:S(2)}) collective-permute-start(bf16[8,256,128]{2,1,0:T(8,128)(2,1)S(1)} %get-tuple-element.23.refs_0_), channel_id=1, source_target_pairs={{0,4},{1,5},{2,66},{3,67},{4,8},{5,9},{6,70},{7,71},{8,12},{9,13},... | collective-permute-start | bytes 1572872 | tf_op jit(solution)/shard_map/ppermute | solution.py:33
  35.8 9.2 %collective-permute-start.11 = (bf16[8,256,128]{2,1,0:T(8,128)(2,1)S(1)}, bf16[8,256,128]{2,1,0:T(8,128)(2,1)S(1)}, u32[]{:S(2)}, u32[]{:S(2)}) collective-permute-start(bf16[8,256,128]{2,1,0:T(8,128)(2,1)S(1)} %get-tuple-element.24.refs_1_), channel_id=1, source_target_pairs={{0,28},{1,29},{2,194},{3,195},{4,0},{5,1},{6,198},{7,199},{8,4},{9... | collective-permute-start | bytes 1572872 | tf_op jit(solution)/shard_map/ppermute | solution.py:33
  38.4 16.6 %collective-permute-start.13 = (bf16[8,256,128]{2,1,0:T(8,128)(2,1)S(1)}, bf16[8,256,128]{2,1,0:T(8,128)(2,1)S(1)}, u32[]{:S(2)}, u32[]{:S(2)}) collective-permute-start(bf16[8,256,128]{2,1,0:T(8,128)(2,1)S(1)} %get-tuple-element.23.refs_0_), channel_id=1, source_target_pairs={{0,28},{1,29},{2,194},{3,195},{4,0},{5,1},{6,198},{7,199},{8,4},{9... | collective-permute-start | bytes 1572872 | tf_op jit(solution)/shard_map/ppermute | solution.py:33
  38.5 16.5 %collective-permute-start.14 = (bf16[8,256,128]{2,1,0:T(8,128)(2,1)S(1)}, bf16[8,256,128]{2,1,0:T(8,128)(2,1)S(1)}, u32[]{:S(2)}, u32[]{:S(2)}) collective-permute-start(bf16[8,256,128]{2,1,0:T(8,128)(2,1)S(1)} %get-tuple-element.24.refs_1_), channel_id=1, source_target_pairs={{0,4},{1,5},{2,66},{3,67},{4,8},{5,9},{6,70},{7,71},{8,12},{9,13},... | collective-permute-start | bytes 1572872 | tf_op jit(solution)/shard_map/ppermute | solution.py:33
  45.0 12.4 %collective-permute-start.10 = (bf16[8,256,128]{2,1,0:T(8,128)(2,1)S(1)}, bf16[8,256,128]{2,1,0:T(8,128)(2,1)S(1)}, u32[]{:S(2)}, u32[]{:S(2)}) collective-permute-start(bf16[8,256,128]{2,1,0:T(8,128)(2,1)S(1)} %collective-permute-done.9.refs_0_), channel_id=1, source_target_pairs={{0,4},{1,5},{2,66},{3,67},{4,8},{5,9},{6,70},{7,71},{8,12},{9,13},... | collective-permute-start | bytes 1572872 | tf_op jit(solution)/shard_map/ppermute | solution.py:33
  45.0 12.4 %collective-permute-start.12 = (bf16[8,256,128]{2,1,0:T(8,128)(2,1)S(1)}, bf16[8,256,128]{2,1,0:T(8,128)(2,1)S(1)}, u32[]{:S(2)}, u32[]{:S(2)}) collective-permute-start(bf16[8,256,128]{2,1,0:T(8,128)(2,1)S(1)} %collective-permute-done.11.refs_3_), channel_id=1, source_target_pairs={{0,28},{1,29},{2,194},{3,195},{4,0},{5,1},{6,198},{7,199},{8,4},{9... | collective-permute-start | bytes 1572872 | tf_op jit(solution)/shard_map/ppermute | solution.py:33
  47.7 3.4 %copy-start = (bf16[1,512,8192]{2,1,0:T(8,128)(2,1)S(1)}, bf16[1,512,8192]{2,1,0:T(8,128)(2,1)}, u32[]{:S(2)}) copy-start(bf16[1,512,8192]{2,1,0:T(8,128)(2,1)} %param.4) | copy-start | bytes 25165828
  58.7 11.6 %collective-permute-start.15 = (bf16[512,512]{1,0:T(8,128)(2,1)S(1)}, bf16[512,512]{1,0:T(8,128)(2,1)S(1)}, u32[]{:S(2)}, u32[]{:S(2)}) collective-permute-start(bf16[512,512]{1,0:T(8,128)(2,1)S(1)} %shard_map.77), channel_id=1, source_target_pairs={{0,2},{1,3},{2,0},{3,1},{4,6},{5,7},{6,4},{7,5},{8,10},{9,11},{10,... | collective-permute-start | bytes 1572872 | tf_op jit(solution)/shard_map/ppermute | solution.py:33

commit v3 on v2

--- a/solution.py
+++ b/solution.py
@@ -58,14 +58,14 @@
     return lax.rem(value + 4, 4)
 
 
-def call(kernel, out_shape, *, flops=0, size=1, scratch=(), in_specs=None):
+def call(kernel, out_shape, *, flops=0, size=1, scratch=(), in_specs=None, limit=VMEM_LIMIT):
     specs = {} if in_specs is None else {"in_specs": in_specs}
     return pl.pallas_call(
         kernel,
         out_shape=out_shape,
         **specs,
         scratch_shapes=list(scratch),
-        compiler_params=pltpu.CompilerParams(vmem_limit_bytes=VMEM_LIMIT),
+        compiler_params=pltpu.CompilerParams(vmem_limit_bytes=limit),
         cost_estimate=pl.CostEstimate(flops=flops, bytes_accessed=size, transcendentals=0),
     )
 
@@ -127,28 +127,39 @@
             high[pl.ds(row, 4)] = piece[...]
 
 
-def pack_kernel(own, other, out, sems):
+def pack_kernel(tokens, out, sems):
     _, _, _, c = position()
     copies = []
-    for side, tokens in enumerate((own, other)):
-        for near in range(4):
-            for pair in range(4):
-                row = (pair % 2) * 16 + ((pair // 2) * 4 + near) * 2
-                source = pl.multiple_of((row + c) * 256, 256)
-                copies.append(
-                    pltpu.make_async_copy(
-                        tokens.at[:, pl.ds(source, 256)],
-                        out.at[pl.ds(side * 512, 512), pl.ds((near * 4 + pair) * 256, 256)],
-                        sems.at[len(copies)],
-                    )
+    for near in range(4):
+        for pair in range(4):
+            row = (pair % 2) * 16 + ((pair // 2) * 4 + near) * 2
+            source = pl.multiple_of((row + c) * 256, 256)
+            copies.append(
+                pltpu.make_async_copy(
+                    tokens.at[:, pl.ds(source, 256)],
+                    out.at[:, pl.ds((near * 4 + pair) * 256, 256)],
+                    sems.at[len(copies)],
                 )
+            )
     for copy in copies:
         copy.start()
     for copy in copies:
         copy.wait()
 
 
-def product_kernel(steps, sides, has_start, packed, *refs):
+def pack(tokens, space, limit):
+    return call(
+        pack_kernel,
+        jax.ShapeDtypeStruct((512, 4096), jnp.bfloat16),
+        size=2**23,
+        scratch=(pltpu.SemaphoreType.DMA((16,)),),
+        in_specs=[pl.BlockSpec(memory_space=space)],
+        limit=limit,
+    )(tokens)
+
+
+def product_kernel(steps, sides, has_start, *refs):
+    packed, refs = refs[: len(sides)], refs[len(sides) :]
     count = len(steps)
     lows, highs = refs[:count], refs[count : 2 * count]
     starts = refs[2 * count : 2 * count + len(sides)] if has_start else (None,) * len(sides)
@@ -157,26 +168,24 @@
 
     @pl.when(c == 0)
     def _():
-        for side, start, out in zip(sides, starts, outs):
-            rows = pl.ds(side * 512, 512)
+        for rows, start, out in zip(packed, starts, outs):
             for half, pieces in enumerate((lows, highs)):
                 columns = pl.ds(half * 256, 256)
                 total = start[:, columns] if has_start else None
                 for step, piece in zip(steps, pieces):
                     near = pl.multiple_of(wrap(z % 4 - step) * 1024, 1024)
                     block = jnp.concatenate([piece[pl.ds(q * 4, 4)].reshape(1024, 128) for q in range(2)], axis=1)
-                    term = jnp.dot(packed[rows, pl.ds(near, 1024)], block, preferred_element_type=jnp.float32)
+                    term = jnp.dot(rows[:, pl.ds(near, 1024)], block, preferred_element_type=jnp.float32)
                     total = term if total is None else total + term
                 out[:, columns] = total.astype(out.dtype)
 
     @pl.when(c == 1)
     def _():
-        for side, start, out in zip(sides, starts, outs):
-            rows = pl.ds(side * 512, 512)
+        for rows, start, out in zip(packed, starts, outs):
             total = None
             for half, pieces in enumerate((lows, highs)):
                 block = jnp.concatenate([piece[...].reshape(2048, 128) for piece in pieces], axis=1)
-                term = jnp.dot(packed[rows, pl.ds(half * 2048, 2048)], block, preferred_element_type=jnp.float32)
+                term = jnp.dot(rows[:, pl.ds(half * 2048, 2048)], block, preferred_element_type=jnp.float32)
                 total = term if total is None else total + term
             if has_start:
                 out[...] = start[...].astype(out.dtype)
@@ -192,7 +201,7 @@
         (jax.ShapeDtypeStruct((512, 512), dtype),) * len(sides),
         flops=2 * count * 512 * 1024 * 512,
         size=count * 2**20,
-    )(packed, *lows, *highs, *starts)
+    )(*[packed[side] for side in sides], *lows, *highs, *starts)
 
 
 def per_device(tokens, pseudo_grad, anchor, momentum):
@@ -211,20 +220,19 @@
     by_y = send(weights, lambda x, y, z, c: (x, y + 1, z, c))
     (two,) = call(join_y_kernel, (blocks(2),), size=2**18)(weights, by_y)
     by_far = send(two, lambda x, y, z, c: (x, y, z + 4, c))
+    packed_own = pack(own_tokens, pltpu.HBM, 44 * 1024 * 1024)
+    two, packed_own = lax.optimization_barrier((two, packed_own))
     (four,) = call(join_far_kernel, (blocks(4),), size=2**19)(two, by_far)
     fours = [send(four, early(step)) for step in STEPS]
+    packed_other = pack(other_tokens, pltpu.VMEM, VMEM_LIMIT)
+    four, packed_other = lax.optimization_barrier((four, packed_other))
+    packed = (packed_own, packed_other)
     low, high = call(join_four_kernel, (blocks(8), blocks(8)), size=2**21)(four, *fours)
-    (packed,) = call(
-        pack_kernel,
-        (jax.ShapeDtypeStruct((1024, 4096), jnp.bfloat16),),
-        size=2**24,
-        scratch=(pltpu.SemaphoreType.DMA((32,)),),
-        in_specs=[pl.BlockSpec(memory_space=pl.ANY), pl.BlockSpec(memory_space=pltpu.VMEM)],
-    )(own_tokens, other_tokens)
     low_up, high_down = send(low, late(1)), send(high, late(-1))
     high_up, low_down = send(high, late(1)), send(low, late(-1))
+    starts = product(packed, (0,), (low,), (high,), (0, 1))
+    low_up, high_down, *starts = lax.optimization_barrier((low_up, high_down, *starts))
     low_two, high_two = send(low_up, late(1)), send(high_down, late(-1))
-    starts = product(packed, (0,), (low,), (high,), (0, 1))
     starts = product(packed, (1, -1), (low_up, low_down), (high_up, high_down), (0, 1), starts)
     (away,) = product(packed, (2,), (low_two,), (high_two,), (1,), starts[1:], jnp.bfloat16)
     returned = send(away, lambda x, y, z, c: (x, y, z, c + 1))

time: 71.4 us -> 71.4 us (level)
  the two profiles are of different devices: /device:TPU:113 before, /device:TPU:1 now
where the time goes in v3:
time: 71.4 us; the launch traced here: 70 us
  starting transfers between devices  31.5 us (44%)
  waiting for transfers between devices  22.7 us (32%)
  Pallas kernels  11.3 us (16%)
  local copies, waits for them, and re-layouts  2.76 us (4%)
  other arithmetic  0.95 us (1%)
  between operations  0.74 us (1%)
    ppermute x16, starting transfers between devices, send(): return lax.ppermute(value, AXES, pairs(move))  31.5 us
    ppermute x16, waiting for transfers between devices, send(): return lax.ppermute(value, AXES, pairs(move))  22.7 us
    pallas_call x4, Pallas kernels, product(): call(functools.partial(product_kernel, steps, sides, bool(starts)), (jax....  7.13 us
    pallas_call x2, Pallas kernels, pack(): call(pack_kernel, jax.ShapeDtypeStruct((512, 4096), jnp.bfloat16), size=2...  3.13 us
    unnamed x6, local copies, waits for them, and re-layouts  2.76 us
  transfers between devices with their start and end apart: 16, of which 11 were waited for; matrix products, arithmetic and copies ran while one was open for 0% of the time, Pallas kernels for 14%

profile of v3, /device:TPU:1, one launch (start us, length us, event | category | flops | bytes accessed | tf_op | source)
XLA Modules:
  0.0 70.0 jit_solution(6405412490503079556)
XLA Ops:
  0.6 3.3 %collective-permute-start.5 = (bf16[512,8192]{1,0:T(8,128)(2,1)}, bf16[512,8192]{1,0:T(8,128)(2,1)S(1)}, u32[]{:S(2)}, u32[]{:S(2)}) collective-permute-start(bf16[512,8192]{1,0:T(8,128)(2,1)} %bitcast.15), channel_id=1, source_target_pairs={{0,2},{1,3},{2,0},{3,1},{4,6},{5,7},{6,4},{7,5},{8,10},{9,11},{10,... | collective-permute-start | bytes 25165832 | tf_op jit(solution)/shard_map/ppermute | solution.py:33
  4.0 0.0 copy-start
  4.0 0.9 %copy-done = bf16[1,256,512]{2,1,0:T(8,128)(2,1)S(1)} copy-done((bf16[1,256,512]{2,1,0:T(8,128)(2,1)S(1)}, bf16[1,256,512]{2,1,0:T(8,128)(2,1)}, u32[]{:S(2)}) %copy-start) | copy-done | bytes 262168
  5.0 0.1 collective-permute-start
  5.1 2.7 %collective-permute-start.1 = (bf16[256,128]{1,0:T(8,128)(2,1)S(1)}, bf16[256,128]{1,0:T(8,128)(2,1)S(1)}, u32[]{:S(2)}, u32[]{:S(2)}) collective-permute-start(bf16[256,128]{1,0:T(8,128)(2,1)S(1)} %get-tuple-element.27), channel_id=1, source_target_pairs={{0,192},{1,193},{2,194},{3,195},{4,196},{5,197},{6,198},{7,199},{8... | collective-permute-start | bytes 196616 | tf_op jit(solution)/shard_map/ppermute | solution.py:33
  7.7 0.0 collective-permute-start.2
  7.7 0.0 copy-start.1
  7.7 0.9 %copy-done.1 = f32[256,1,1,128]{3,2,1,0:T(1,128)S(1)} copy-done((f32[256,1,1,128]{3,2,1,0:T(1,128)S(1)}, f32[256,1,1,128]{3,2,1,0:T(1,128)}, u32[]{:S(2)}) %copy-start.1) | copy-done | bytes 131096
  8.6 0.0 copy-start.2
  8.6 0.9 %copy-done.2 = f32[256,1,1,128]{3,2,1,0:T(1,128)S(1)} copy-done((f32[256,1,1,128]{3,2,1,0:T(1,128)S(1)}, f32[256,1,1,128]{3,2,1,0:T(1,128)}, u32[]{:S(2)}) %copy-start.2) | copy-done | bytes 131096
  9.6 0.4 collective-permute-done.one
  10.0 0.6 collective-permute-done.1.two
  10.5 1.8 %collective-permute-done.2.three = bf16[256,128]{1,0:T(8,128)(2,1)S(1)} collective-permute-done((bf16[256,128]{1,0:T(8,128)(2,1)S(1)}, bf16[256,128]{1,0:T(8,128)(2,1)S(1)}, u32[]{:S(2)}, u32[]{:S(2)}) %collective-permute-start.2) | collective-permute-done | bytes 65568 | tf_op jit(solution)/shard_map/ppermute | solution.py:33
  12.3 0.1 shard_map.69.own
  12.4 1.3 %collective-permute-start.3 = (bf16[256,128]{1,0:T(8,128)(2,1)S(1)}, bf16[256,128]{1,0:T(8,128)(2,1)S(1)}, u32[]{:S(2)}, u32[]{:S(2)}) collective-permute-start(bf16[256,128]{1,0:T(8,128)(2,1)S(1)} %shard_map.69.own), channel_id=1, source_target_pairs={{0,32},{1,33},{2,34},{3,35},{4,36},{5,37},{6,38},{7,39},{8,40},{9,... | collective-permute-start | bytes 196616 | tf_op jit(solution)/shard_map/ppermute | solution.py:33
  13.7 3.4 %collective-permute-done.3.other = bf16[256,128]{1,0:T(8,128)(2,1)S(1)} collective-permute-done((bf16[256,128]{1,0:T(8,128)(2,1)S(1)}, bf16[256,128]{1,0:T(8,128)(2,1)S(1)}, u32[]{:S(2)}, u32[]{:S(2)}) %collective-permute-start.3) | collective-permute-done | bytes 65568 | tf_op jit(solution)/shard_map/ppermute | solution.py:33
  17.1 5.3 %collective-permute-start.4 = (bf16[2,256,128]{2,1,0:T(8,128)(2,1)S(1)}, bf16[2,256,128]{2,1,0:T(8,128)(2,1)S(1)}, u32[]{:S(2)}, u32[]{:S(2)}) collective-permute-start(bf16[2,256,128]{2,1,0:T(8,128)(2,1)S(1)} %shard_map.70.own), channel_id=1, source_target_pairs={{0,16},{1,17},{2,18},{3,19},{4,20},{5,21},{6,22},{7,23},{8,24},{9,... | collective-permute-start | bytes 393224 | tf_op jit(solution)/shard_map/ppermute | solution.py:33
  22.4 2.3 %shard_map.71.refs_0_ = bf16[512,4096]{1,0:T(8,128)(2,1)S(1)} custom-call(bf16[512,8192]{1,0:T(8,128)(2,1)} %bitcast.16), custom_call_target="tpu_custom_call" | custom-call | bytes 8388608 | tf_op jit(solution)/shard_map/pallas_call | solution.py:151
  24.7 0.3 collective-permute-done.4.other
  25.1 0.5 collective-permute-start.6
  25.6 3.7 %collective-permute-start.7 = (bf16[4,256,128]{2,1,0:T(8,128)(2,1)S(1)}, bf16[4,256,128]{2,1,0:T(8,128)(2,1)S(1)}, u32[]{:S(2)}, u32[]{:S(2)}) collective-permute-start(bf16[4,256,128]{2,1,0:T(8,128)(2,1)S(1)} %shard_map.72.own), channel_id=1, source_target_pairs={{0,192},{1,193},{2,30},{3,31},{4,196},{5,197},{6,2},{7,3},{8,200},... | collective-permute-start | bytes 786440 | tf_op jit(solution)/shard_map/ppermute | solution.py:33
  29.3 0.0 collective-permute-start.8
  29.3 0.0 collective-permute-done.5.tokens
  29.3 0.8 %shard_map.73.refs_1_.refs_0_ = bf16[512,4096]{1,0:T(8,128)(2,1)S(1)} custom-call(bf16[512,8192]{1,0:T(8,128)(2,1)S(1)} %collective-permute-done.5.tokens), custom_call_target="tpu_custom_call" | custom-call | bytes 8388608 | tf_op jit(solution)/shard_map/pallas_call | solution.py:151
  30.1 2.9 %collective-permute-done.6.one = bf16[4,256,128]{2,1,0:T(8,128)(2,1)S(1)} collective-permute-done((bf16[4,256,128]{2,1,0:T(8,128)(2,1)S(1)}, bf16[4,256,128]{2,1,0:T(8,128)(2,1)S(1)}, u32[]{:S(2)}, u32[]{:S(2)}) %collective-permute-start.6) | collective-permute-done | bytes 262176 | tf_op jit(solution)/shard_map/ppermute | solution.py:33
  33.0 0.0 collective-permute-done.7.two
  33.0 4.3 %collective-permute-done.8.three = bf16[4,256,128]{2,1,0:T(8,128)(2,1)S(1)} collective-permute-done((bf16[4,256,128]{2,1,0:T(8,128)(2,1)S(1)}, bf16[4,256,128]{2,1,0:T(8,128)(2,1)S(1)}, u32[]{:S(2)}, u32[]{:S(2)}) %collective-permute-start.8) | collective-permute-done | bytes 262176 | tf_op jit(solution)/shard_map/ppermute | solution.py:33
  37.3 0.1 shard_map.74
  37.4 0.3 collective-permute-start.9
  37.8 2.4 %collective-permute-start.10 = (bf16[8,256,128]{2,1,0:T(8,128)(2,1)S(1)}, bf16[8,256,128]{2,1,0:T(8,128)(2,1)S(1)}, u32[]{:S(2)}, u32[]{:S(2)}) collective-permute-start(bf16[8,256,128]{2,1,0:T(8,128)(2,1)S(1)} %get-tuple-element.35.refs_3_), channel_id=1, source_target_pairs={{0,28},{1,29},{2,194},{3,195},{4,0},{5,1},{6,198},{7,199},{8,4},{9... | collective-permute-start | bytes 1572872 | tf_op jit(solution)/shard_map/ppermute | solution.py:33
  40.2 0.0 collective-permute-start.13
  40.2 1.4 %collective-permute-start.14 = (bf16[8,256,128]{2,1,0:T(8,128)(2,1)S(1)}, bf16[8,256,128]{2,1,0:T(8,128)(2,1)S(1)}, u32[]{:S(2)}, u32[]{:S(2)}) collective-permute-start(bf16[8,256,128]{2,1,0:T(8,128)(2,1)S(1)} %get-tuple-element.35.refs_3_), channel_id=1, source_target_pairs={{0,4},{1,5},{2,66},{3,67},{4,8},{5,9},{6,70},{7,71},{8,12},{9,13},... | collective-permute-start | bytes 1572872 | tf_op jit(solution)/shard_map/ppermute | solution.py:33
  41.7 2.3 %shard_map.75 = (f32[512,512]{1,0:T(8,128)S(1)}, f32[512,512]{1,0:T(8,128)S(1)}) custom-call(bf16[512,4096]{1,0:T(8,128)(2,1)S(1)} %shard_map.71.refs_0_, bf16[512,4096]{1,0:T(8,128)(2,1)S(1)} %shard_map.73.refs_1_.refs_0_, bf16[8,256,128]{2,1,0:T(8,128)(2,1)S(1)} %get-tuple-element.34.refs_2_, bf16[8,256,128]{2,1,0:T(8,128)(2,1)S(1)} %get-tuple-element.35.refs_3_), custom_call_target="tpu_custom_call" | custom-call | flops 1073741824 | bytes 2097152 | tf_op jit(solution)/shard_map/pallas_call | solution.py:199
  44.0 2.8 %collective-permute-done.9.refs_2_ = bf16[8,256,128]{2,1,0:T(8,128)(2,1)S(1)} collective-permute-done((bf16[8,256,128]{2,1,0:T(8,128)(2,1)S(1)}, bf16[8,256,128]{2,1,0:T(8,128)(2,1)S(1)}, u32[]{:S(2)}, u32[]{:S(2)}) %collective-permute-start.9) | collective-permute-done | bytes 524320 | tf_op jit(solution)/shard_map/ppermute | solution.py:33
  46.8 0.0 collective-permute-done.10.refs_5_
  46.8 0.3 collective-permute-start.11
  47.0 2.7 %collective-permute-start.12 = (bf16[8,256,128]{2,1,0:T(8,128)(2,1)S(1)}, bf16[8,256,128]{2,1,0:T(8,128)(2,1)S(1)}, u32[]{:S(2)}, u32[]{:S(2)}) collective-permute-start(bf16[8,256,128]{2,1,0:T(8,128)(2,1)S(1)} %collective-permute-done.10.refs_5_), channel_id=1, source_target_pairs={{0,28},{1,29},{2,194},{3,195},{4,0},{5,1},{6,198},{7,199},{8,4},{9... | collective-permute-start | bytes 1572872 | tf_op jit(solution)/shard_map/ppermute | solution.py:33
  49.7 2.2 %collective-permute-done.13.refs_3_ = bf16[8,256,128]{2,1,0:T(8,128)(2,1)S(1)} collective-permute-done((bf16[8,256,128]{2,1,0:T(8,128)(2,1)S(1)}, bf16[8,256,128]{2,1,0:T(8,128)(2,1)S(1)}, u32[]{:S(2)}, u32[]{:S(2)}) %collective-permute-start.13) | collective-permute-done | bytes 524320 | tf_op jit(solution)/shard_map/ppermute | solution.py:33
  51.9 0.7 %collective-permute-done.14.refs_4_ = bf16[8,256,128]{2,1,0:T(8,128)(2,1)S(1)} collective-permute-done((bf16[8,256,128]{2,1,0:T(8,128)(2,1)S(1)}, bf16[8,256,128]{2,1,0:T(8,128)(2,1)S(1)}, u32[]{:S(2)}, u32[]{:S(2)}) %collective-permute-start.14) | collective-permute-done | bytes 524320 | tf_op jit(solution)/shard_map/ppermute | solution.py:33
  52.7 2.3 %shard_map.76 = (f32[512,512]{1,0:T(8,128)S(1)}, f32[512,512]{1,0:T(8,128)S(1)}) custom-call(bf16[512,4096]{1,0:T(8,128)(2,1)S(1)} %shard_map.71.refs_0_, bf16[512,4096]{1,0:T(8,128)(2,1)S(1)} %shard_map.73.refs_1_.refs_0_, bf16[8,256,128]{2,1,0:T(8,128)(2,1)S(1)} %collective-permute-done.9.refs_2_, ...), custom_call_target="tpu_custom_call" | custom-call | flops 2147483648 | bytes 4194304 | tf_op jit(solution)/shard_map/pallas_call | solution.py:199
  55.0 3.3 %collective-permute-done.11.refs_1_ = bf16[8,256,128]{2,1,0:T(8,128)(2,1)S(1)} collective-permute-done((bf16[8,256,128]{2,1,0:T(8,128)(2,1)S(1)}, bf16[8,256,128]{2,1,0:T(8,128)(2,1)S(1)}, u32[]{:S(2)}, u32[]{:S(2)}) %collective-permute-start.11) | collective-permute-done | bytes 524320 | tf_op jit(solution)/shard_map/ppermute | solution.py:33
  58.3 0.0 collective-permute-done.12.refs_2_
  58.3 1.2 %shard_map.78 = bf16[512,512]{1,0:T(8,128)(2,1)S(1)} custom-call(bf16[512,4096]{1,0:T(8,128)(2,1)S(1)} %shard_map.73.refs_1_.refs_0_, bf16[8,256,128]{2,1,0:T(8,128)(2,1)S(1)} %collective-permute-done.11.refs_1_, bf16[8,256,128]{2,1,0:T(8,128)(2,1)S(1)} %collective-permute-done.12.refs_2_, f32[512,512]{1,0:T(8,128)S(1)} %get-tuple-element.44.refs_3_), custom_call_target="tpu_custom_call" | custom-call | flops 536870912 | bytes 1048576 | tf_op jit(solution)/shard_map/pallas_call | solution.py:199
  59.5 7.5 %collective-permute-start.15 = (bf16[512,512]{1,0:T(8,128)(2,1)S(1)}, bf16[512,512]{1,0:T(8,128)(2,1)S(1)}, u32[]{:S(2)}, u32[]{:S(2)}) collective-permute-start(bf16[512,512]{1,0:T(8,128)(2,1)S(1)} %shard_map.78), channel_id=1, source_target_pairs={{0,2},{1,3},{2,0},{3,1},{4,6},{5,7},{6,4},{7,5},{8,10},{9,11},{10,... | collective-permute-start | bytes 1572872 | tf_op jit(solution)/shard_map/ppermute | solution.py:33
  67.0 0.8 %shard_map.79 = (f32[256,128]{1,0:T(8,128)}, f32[256,128]{1,0:T(8,128)}) custom-call(bf16[256,128]{1,0:T(8,128)(2,1)S(1)} %get-tuple-element.25.own, bf16[256,128]{1,0:T(8,128)(2,1)S(1)} %collective-permute-done.one, bf16[256,128]{1,0:T(8,128)(2,1)S(1)} %collective-permute-done.1.two, bf16[256,128]{1,0:T(8,128)(2,1)S(1)} %collective-permute-done.2.three, ...), custom_call_target="tpu_custom_call" | custom-call | bytes 1048576 | tf_op jit(solution)/shard_map/pallas_call | solution.py:219
  67.8 1.2 %shard_map.77 = f32[512,512]{1,0:T(8,128)S(1)} custom-call(bf16[512,4096]{1,0:T(8,128)(2,1)S(1)} %shard_map.71.refs_0_, bf16[8,256,128]{2,1,0:T(8,128)(2,1)S(1)} %collective-permute-done.11.refs_1_, bf16[8,256,128]{2,1,0:T(8,128)(2,1)S(1)} %collective-permute-done.12.refs_2_, f32[512,512]{1,0:T(8,128)S(1)} %get-tuple-element.43.refs_3_), custom_call_target="tpu_custom_call" | custom-call | flops 536870912 | bytes 1048576 | tf_op jit(solution)/shard_map/pallas_call | solution.py:199
  69.0 0.0 collective-permute-done.15
  69.0 1.0 %fusion = bf16[1,512,512]{2,1,0:T(8,128)(2,1)} fusion(f32[512,512]{1,0:T(8,128)S(1)} %shard_map.77, bf16[512,512]{1,0:T(8,128)(2,1)S(1)} %collective-permute-done.15), kind=kLoop, calls=%fused_computation.1 | loop fusion | flops 786432 | bytes 2097152 | tf_op jit(solution)/shard_map/broadcast_in_dim | solution.py:240
  (4 shorter events, 0.1 us)
Async XLA Ops:
  0.6 28.7 %collective-permute-start.5 = (bf16[512,8192]{1,0:T(8,128)(2,1)}, bf16[512,8192]{1,0:T(8,128)(2,1)S(1)}, u32[]{:S(2)}, u32[]{:S(2)}) collective-permute-start(bf16[512,8192]{1,0:T(8,128)(2,1)} %bitcast.15), channel_id=1, source_target_pairs={{0,2},{1,3},{2,0},{3,1},{4,6},{5,7},{6,4},{7,5},{8,10},{9,11},{10,... | collective-permute-start | bytes 25165832 | tf_op jit(solution)/shard_map/ppermute | solution.py:33
  4.0 0.9 %copy-start = (bf16[1,256,512]{2,1,0:T(8,128)(2,1)S(1)}, bf16[1,256,512]{2,1,0:T(8,128)(2,1)}, u32[]{:S(2)}) copy-start(bf16[1,256,512]{2,1,0:T(8,128)(2,1)} %param.5) | copy-start | bytes 786436
  5.0 5.0 %collective-permute-start = (bf16[256,128]{1,0:T(8,128)(2,1)S(1)}, bf16[256,128]{1,0:T(8,128)(2,1)S(1)}, u32[]{:S(2)}, u32[]{:S(2)}) collective-permute-start(bf16[256,128]{1,0:T(8,128)(2,1)S(1)} %get-tuple-element.26), channel_id=1, source_target_pairs={{0,64},{1,65},{2,66},{3,67},{4,68},{5,69},{6,70},{7,71},{8,72},{9,... | collective-permute-start | bytes 196616 | tf_op jit(solution)/shard_map/ppermute | solution.py:33
  5.1 5.5 %collective-permute-start.1 = (bf16[256,128]{1,0:T(8,128)(2,1)S(1)}, bf16[256,128]{1,0:T(8,128)(2,1)S(1)}, u32[]{:S(2)}, u32[]{:S(2)}) collective-permute-start(bf16[256,128]{1,0:T(8,128)(2,1)S(1)} %get-tuple-element.27), channel_id=1, source_target_pairs={{0,192},{1,193},{2,194},{3,195},{4,196},{5,197},{6,198},{7,199},{8... | collective-permute-start | bytes 196616 | tf_op jit(solution)/shard_map/ppermute | solution.py:33
  7.7 4.6 %collective-permute-start.2 = (bf16[256,128]{1,0:T(8,128)(2,1)S(1)}, bf16[256,128]{1,0:T(8,128)(2,1)S(1)}, u32[]{:S(2)}, u32[]{:S(2)}) collective-permute-start(bf16[256,128]{1,0:T(8,128)(2,1)S(1)} %get-tuple-element.28), channel_id=1, source_target_pairs={{0,128},{1,129},{2,130},{3,131},{4,132},{5,133},{6,134},{7,135},{8... | collective-permute-start | bytes 196616 | tf_op jit(solution)/shard_map/ppermute | solution.py:33
  7.7 0.9 %copy-start.1 = (f32[256,1,1,128]{3,2,1,0:T(1,128)S(1)}, f32[256,1,1,128]{3,2,1,0:T(1,128)}, u32[]{:S(2)}) copy-start(f32[256,1,1,128]{3,2,1,0:T(1,128)} %param.6) | copy-start | bytes 393220
  8.6 0.9 %copy-start.2 = (f32[256,1,1,128]{3,2,1,0:T(1,128)S(1)}, f32[256,1,1,128]{3,2,1,0:T(1,128)}, u32[]{:S(2)}) copy-start(f32[256,1,1,128]{3,2,1,0:T(1,128)} %param.7) | copy-start | bytes 393220
  12.4 4.7 %collective-permute-start.3 = (bf16[256,128]{1,0:T(8,128)(2,1)S(1)}, bf16[256,128]{1,0:T(8,128)(2,1)S(1)}, u32[]{:S(2)}, u32[]{:S(2)}) collective-permute-start(bf16[256,128]{1,0:T(8,128)(2,1)S(1)} %shard_map.69.own), channel_id=1, source_target_pairs={{0,32},{1,33},{2,34},{3,35},{4,36},{5,37},{6,38},{7,39},{8,40},{9,... | collective-permute-start | bytes 196616 | tf_op jit(solution)/shard_map/ppermute | solution.py:33
  17.1 7.9 %collective-permute-start.4 = (bf16[2,256,128]{2,1,0:T(8,128)(2,1)S(1)}, bf16[2,256,128]{2,1,0:T(8,128)(2,1)S(1)}, u32[]{:S(2)}, u32[]{:S(2)}) collective-permute-start(bf16[2,256,128]{2,1,0:T(8,128)(2,1)S(1)} %shard_map.70.own), channel_id=1, source_target_pairs={{0,16},{1,17},{2,18},{3,19},{4,20},{5,21},{6,22},{7,23},{8,24},{9,... | collective-permute-start | bytes 393224 | tf_op jit(solution)/shard_map/ppermute | solution.py:33
  25.1 7.9 %collective-permute-start.6 = (bf16[4,256,128]{2,1,0:T(8,128)(2,1)S(1)}, bf16[4,256,128]{2,1,0:T(8,128)(2,1)S(1)}, u32[]{:S(2)}, u32[]{:S(2)}) collective-permute-start(bf16[4,256,128]{2,1,0:T(8,128)(2,1)S(1)} %shard_map.72.own), channel_id=1, source_target_pairs={{0,64},{1,65},{2,6},{3,7},{4,68},{5,69},{6,10},{7,11},{8,72},{9,73... | collective-permute-start | bytes 786440 | tf_op jit(solution)/shard_map/ppermute | solution.py:33
  25.6 7.4 %collective-permute-start.7 = (bf16[4,256,128]{2,1,0:T(8,128)(2,1)S(1)}, bf16[4,256,128]{2,1,0:T(8,128)(2,1)S(1)}, u32[]{:S(2)}, u32[]{:S(2)}) collective-permute-start(bf16[4,256,128]{2,1,0:T(8,128)(2,1)S(1)} %shard_map.72.own), channel_id=1, source_target_pairs={{0,192},{1,193},{2,30},{3,31},{4,196},{5,197},{6,2},{7,3},{8,200},... | collective-permute-start | bytes 786440 | tf_op jit(solution)/shard_map/ppermute | solution.py:33
  29.3 8.0 %collective-permute-start.8 = (bf16[4,256,128]{2,1,0:T(8,128)(2,1)S(1)}, bf16[4,256,128]{2,1,0:T(8,128)(2,1)S(1)}, u32[]{:S(2)}, u32[]{:S(2)}) collective-permute-start(bf16[4,256,128]{2,1,0:T(8,128)(2,1)S(1)} %shard_map.72.own), channel_id=1, source_target_pairs={{0,128},{1,129},{2,10},{3,11},{4,132},{5,133},{6,30},{7,31},{8,136... | collective-permute-start | bytes 786440 | tf_op jit(solution)/shard_map/ppermute | solution.py:33
  37.4 9.3 %collective-permute-start.9 = (bf16[8,256,128]{2,1,0:T(8,128)(2,1)S(1)}, bf16[8,256,128]{2,1,0:T(8,128)(2,1)S(1)}, u32[]{:S(2)}, u32[]{:S(2)}) collective-permute-start(bf16[8,256,128]{2,1,0:T(8,128)(2,1)S(1)} %get-tuple-element.34.refs_2_), channel_id=1, source_target_pairs={{0,4},{1,5},{2,66},{3,67},{4,8},{5,9},{6,70},{7,71},{8,12},{9,13},... | collective-permute-start | bytes 1572872 | tf_op jit(solution)/shard_map/ppermute | solution.py:33
  37.8 9.0 %collective-permute-start.10 = (bf16[8,256,128]{2,1,0:T(8,128)(2,1)S(1)}, bf16[8,256,128]{2,1,0:T(8,128)(2,1)S(1)}, u32[]{:S(2)}, u32[]{:S(2)}) collective-permute-start(bf16[8,256,128]{2,1,0:T(8,128)(2,1)S(1)} %get-tuple-element.35.refs_3_), channel_id=1, source_target_pairs={{0,28},{1,29},{2,194},{3,195},{4,0},{5,1},{6,198},{7,199},{8,4},{9... | collective-permute-start | bytes 1572872 | tf_op jit(solution)/shard_map/ppermute | solution.py:33
  40.2 11.7 %collective-permute-start.13 = (bf16[8,256,128]{2,1,0:T(8,128)(2,1)S(1)}, bf16[8,256,128]{2,1,0:T(8,128)(2,1)S(1)}, u32[]{:S(2)}, u32[]{:S(2)}) collective-permute-start(bf16[8,256,128]{2,1,0:T(8,128)(2,1)S(1)} %get-tuple-element.34.refs_2_), channel_id=1, source_target_pairs={{0,28},{1,29},{2,194},{3,195},{4,0},{5,1},{6,198},{7,199},{8,4},{9... | collective-permute-start | bytes 1572872 | tf_op jit(solution)/shard_map/ppermute | solution.py:33
  40.2 12.4 %collective-permute-start.14 = (bf16[8,256,128]{2,1,0:T(8,128)(2,1)S(1)}, bf16[8,256,128]{2,1,0:T(8,128)(2,1)S(1)}, u32[]{:S(2)}, u32[]{:S(2)}) collective-permute-start(bf16[8,256,128]{2,1,0:T(8,128)(2,1)S(1)} %get-tuple-element.35.refs_3_), channel_id=1, source_target_pairs={{0,4},{1,5},{2,66},{3,67},{4,8},{5,9},{6,70},{7,71},{8,12},{9,13},... | collective-permute-start | bytes 1572872 | tf_op jit(solution)/shard_map/ppermute | solution.py:33
  46.8 11.5 %collective-permute-start.11 = (bf16[8,256,128]{2,1,0:T(8,128)(2,1)S(1)}, bf16[8,256,128]{2,1,0:T(8,128)(2,1)S(1)}, u32[]{:S(2)}, u32[]{:S(2)}) collective-permute-start(bf16[8,256,128]{2,1,0:T(8,128)(2,1)S(1)} %collective-permute-done.9.refs_2_), channel_id=1, source_target_pairs={{0,4},{1,5},{2,66},{3,67},{4,8},{5,9},{6,70},{7,71},{8,12},{9,13},... | collective-permute-start | bytes 1572872 | tf_op jit(solution)/shard_map/ppermute | solution.py:33
  47.0 11.3 %collective-permute-start.12 = (bf16[8,256,128]{2,1,0:T(8,128)(2,1)S(1)}, bf16[8,256,128]{2,1,0:T(8,128)(2,1)S(1)}, u32[]{:S(2)}, u32[]{:S(2)}) collective-permute-start(bf16[8,256,128]{2,1,0:T(8,128)(2,1)S(1)} %collective-permute-done.10.refs_5_), channel_id=1, source_target_pairs={{0,28},{1,29},{2,194},{3,195},{4,0},{5,1},{6,198},{7,199},{8,4},{9... | collective-permute-start | bytes 1572872 | tf_op jit(solution)/shard_map/ppermute | solution.py:33
  59.5 9.5 %collective-permute-start.15 = (bf16[512,512]{1,0:T(8,128)(2,1)S(1)}, bf16[512,512]{1,0:T(8,128)(2,1)S(1)}, u32[]{:S(2)}, u32[]{:S(2)}) collective-permute-start(bf16[512,512]{1,0:T(8,128)(2,1)S(1)} %shard_map.78), channel_id=1, source_target_pairs={{0,2},{1,3},{2,0},{3,1},{4,6},{5,7},{6,4},{7,5},{8,10},{9,11},{10,... | collective-permute-start | bytes 1572872 | tf_op jit(solution)/shard_map/ppermute | solution.py:33

commit v4 on v3

--- a/solution.py
+++ b/solution.py
@@ -40,13 +40,13 @@
 def early(step):
     def move(x, y, z, c):
         along_z = step if step != 2 or z % 2 == 0 else -step
-        return (x + step, y, z, c) if c == 0 else (x, y, z + along_z, c)
+        return (x + step, y, z, c) if c == 1 else (x, y, z + along_z, c)
 
     return move
 
 
 def late(step):
-    return lambda x, y, z, c: (x, y, z + step, c) if c == 0 else (x + step, y, z, c)
+    return lambda x, y, z, c: (x, y, z + step, c) if c == 1 else (x + step, y, z, c)
 
 
 def position():
@@ -98,22 +98,22 @@
     anchor_new[...], momentum_new[...] = step_of(own, one, two, three, anchor, kept)
 
 
-def join_y_kernel(own, other, out):
-    _, y, _, _ = position()
-    out[y] = own[...]
-    out[1 - y] = other[...]
-
-
 def join_far_kernel(own, other, out):
     _, _, z, _ = position()
     far = z // 4
-    out[pl.ds(far * 2, 2)] = own[...]
-    out[pl.ds((1 - far) * 2, 2)] = other[...]
+    out[far] = own[...]
+    out[1 - far] = other[...]
+
+
+def join_y_kernel(own, other, out):
+    _, y, _, _ = position()
+    out[pl.ds(y * 2, 2)] = own[...]
+    out[pl.ds((1 - y) * 2, 2)] = other[...]
 
 
 def join_four_kernel(own, one, two, three, low, high):
     x, _, z, c = position()
-    here = jnp.where(c == 0, x, z % 4)
+    here = jnp.where(c == 1, x, z % 4)
     for step, piece in zip((0,) + STEPS, (own, one, two, three)):
         place = wrap(here - step)
         row = lax.rem(place, 2) * 4
@@ -132,7 +132,7 @@
     copies = []
     for near in range(4):
         for pair in range(4):
-            row = (pair % 2) * 16 + ((pair // 2) * 4 + near) * 2
+            row = (pair // 2) * 16 + ((pair % 2) * 4 + near) * 2
             source = pl.multiple_of((row + c) * 256, 256)
             copies.append(
                 pltpu.make_async_copy(
@@ -166,7 +166,7 @@
     outs = refs[len(refs) - len(sides) :]
     x, _, z, c = position()
 
-    @pl.when(c == 0)
+    @pl.when(c == 1)
     def _():
         for rows, start, out in zip(packed, starts, outs):
             for half, pieces in enumerate((lows, highs)):
@@ -179,7 +179,7 @@
                     total = term if total is None else total + term
                 out[:, columns] = total.astype(out.dtype)
 
-    @pl.when(c == 1)
+    @pl.when(c == 0)
     def _():
         for rows, start, out in zip(packed, starts, outs):
             total = None
@@ -217,12 +217,12 @@
     prepared = call(prepare_kernel, (state, state), size=2**19)(anchor.reshape(256, 128), momentum.reshape(256, 128))
     (weights,) = call(weights_kernel, (block,), size=2**19)(grads[0], *arrived, *prepared)
     anchor_new, momentum_new = call(state_kernel, (state, state), size=2**20)(grads[0], *arrived, *prepared)
-    by_y = send(weights, lambda x, y, z, c: (x, y + 1, z, c))
-    (two,) = call(join_y_kernel, (blocks(2),), size=2**18)(weights, by_y)
-    by_far = send(two, lambda x, y, z, c: (x, y, z + 4, c))
+    by_far = send(weights, lambda x, y, z, c: (x, y, z + 4, c))
+    (two,) = call(join_far_kernel, (blocks(2),), size=2**18)(weights, by_far)
+    by_y = send(two, lambda x, y, z, c: (x, y + 1, z, c))
     packed_own = pack(own_tokens, pltpu.HBM, 44 * 1024 * 1024)
     two, packed_own = lax.optimization_barrier((two, packed_own))
-    (four,) = call(join_far_kernel, (blocks(4),), size=2**19)(two, by_far)
+    (four,) = call(join_y_kernel, (blocks(4),), size=2**19)(two, by_y)
     fours = [send(four, early(step)) for step in STEPS]
     packed_other = pack(other_tokens, pltpu.VMEM, VMEM_LIMIT)
     four, packed_other = lax.optimization_barrier((four, packed_other))

time: 71.4 us -> 68.1 us (0.954); the launches traced: 70 us -> 67.9 us
  Pallas kernels: 11.3 us -> 9.36 us
    pallas_call x4, Pallas kernels: 7.13 us -> 5.19 us  [product(): call(functools.partial(product_kernel, steps, sides, bool(starts)), (jax....]
  transfers between devices with their start and end apart: 16 -> 16, of which waited for: 11 -> 13; matrix products, arithmetic and copies ran while one was open for 0% -> 0% of each run, Pallas kernels for 14% -> 13%
where the time goes in v4:
time: 68.1 us; the launch traced here: 67.9 us
  starting transfers between devices  31.7 us (47%)
  waiting for transfers between devices  22.4 us (33%)
  Pallas kernels  9.36 us (14%)
  local copies, waits for them, and re-layouts  2.76 us (4%)
  other arithmetic  0.95 us (1%)
  between operations  0.74 us (1%)
    ppermute x16, starting transfers between devices, send(): return lax.ppermute(value, AXES, pairs(move))  31.7 us
    ppermute x16, waiting for transfers between devices, send(): return lax.ppermute(value, AXES, pairs(move))  22.4 us
    pallas_call x4, Pallas kernels, product(): call(functools.partial(product_kernel, steps, sides, bool(starts)), (jax....  5.19 us
    pallas_call x2, Pallas kernels, pack(): call(pack_kernel, jax.ShapeDtypeStruct((512, 4096), jnp.bfloat16), size=2...  3.13 us
    unnamed x6, local copies, waits for them, and re-layouts  2.76 us
  transfers between devices with their start and end apart: 16, of which 13 were waited for; matrix products, arithmetic and copies ran while one was open for 0% of the time, Pallas kernels for 13%

profile of v4, /device:TPU:1, one launch (start us, length us, event | category | flops | bytes accessed | tf_op | source)
XLA Modules:
  0.0 67.9 jit_solution(13866180735961927746)
XLA Ops:
  0.6 3.3 %collective-permute-start.5 = (bf16[512,8192]{1,0:T(8,128)(2,1)}, bf16[512,8192]{1,0:T(8,128)(2,1)S(1)}, u32[]{:S(2)}, u32[]{:S(2)}) collective-permute-start(bf16[512,8192]{1,0:T(8,128)(2,1)} %bitcast.15), channel_id=1, source_target_pairs={{0,2},{1,3},{2,0},{3,1},{4,6},{5,7},{6,4},{7,5},{8,10},{9,11},{10,... | collective-permute-start | bytes 25165832 | tf_op jit(solution)/shard_map/ppermute | solution.py:33
  4.0 0.0 copy-start
  4.0 0.9 %copy-done = bf16[1,256,512]{2,1,0:T(8,128)(2,1)S(1)} copy-done((bf16[1,256,512]{2,1,0:T(8,128)(2,1)S(1)}, bf16[1,256,512]{2,1,0:T(8,128)(2,1)}, u32[]{:S(2)}) %copy-start) | copy-done | bytes 262168
  5.0 0.1 collective-permute-start
  5.1 2.7 %collective-permute-start.1 = (bf16[256,128]{1,0:T(8,128)(2,1)S(1)}, bf16[256,128]{1,0:T(8,128)(2,1)S(1)}, u32[]{:S(2)}, u32[]{:S(2)}) collective-permute-start(bf16[256,128]{1,0:T(8,128)(2,1)S(1)} %get-tuple-element.27), channel_id=1, source_target_pairs={{0,192},{1,193},{2,194},{3,195},{4,196},{5,197},{6,198},{7,199},{8... | collective-permute-start | bytes 196616 | tf_op jit(solution)/shard_map/ppermute | solution.py:33
  7.7 0.0 collective-permute-start.2
  7.7 0.0 copy-start.1
  7.7 0.9 %copy-done.1 = f32[256,1,1,128]{3,2,1,0:T(1,128)S(1)} copy-done((f32[256,1,1,128]{3,2,1,0:T(1,128)S(1)}, f32[256,1,1,128]{3,2,1,0:T(1,128)}, u32[]{:S(2)}) %copy-start.1) | copy-done | bytes 131096
  8.6 0.0 copy-start.2
  8.6 0.9 %copy-done.2 = f32[256,1,1,128]{3,2,1,0:T(1,128)S(1)} copy-done((f32[256,1,1,128]{3,2,1,0:T(1,128)S(1)}, f32[256,1,1,128]{3,2,1,0:T(1,128)}, u32[]{:S(2)}) %copy-start.2) | copy-done | bytes 131096
  9.6 0.4 collective-permute-done.one
  10.0 0.6 collective-permute-done.1.two
  10.5 1.8 %collective-permute-done.2.three = bf16[256,128]{1,0:T(8,128)(2,1)S(1)} collective-permute-done((bf16[256,128]{1,0:T(8,128)(2,1)S(1)}, bf16[256,128]{1,0:T(8,128)(2,1)S(1)}, u32[]{:S(2)}, u32[]{:S(2)}) %collective-permute-start.2) | collective-permute-done | bytes 65568 | tf_op jit(solution)/shard_map/ppermute | solution.py:33
  12.3 0.1 shard_map.69.own
  12.4 5.3 %collective-permute-start.3 = (bf16[256,128]{1,0:T(8,128)(2,1)S(1)}, bf16[256,128]{1,0:T(8,128)(2,1)S(1)}, u32[]{:S(2)}, u32[]{:S(2)}) collective-permute-start(bf16[256,128]{1,0:T(8,128)(2,1)S(1)} %shard_map.69.own), channel_id=1, source_target_pairs={{0,16},{1,17},{2,18},{3,19},{4,20},{5,21},{6,22},{7,23},{8,24},{9,... | collective-permute-start | bytes 196616 | tf_op jit(solution)/shard_map/ppermute | solution.py:33
  17.7 1.8 %collective-permute-done.3.other = bf16[256,128]{1,0:T(8,128)(2,1)S(1)} collective-permute-done((bf16[256,128]{1,0:T(8,128)(2,1)S(1)}, bf16[256,128]{1,0:T(8,128)(2,1)S(1)}, u32[]{:S(2)}, u32[]{:S(2)}) %collective-permute-start.3) | collective-permute-done | bytes 65568 | tf_op jit(solution)/shard_map/ppermute | solution.py:33
  19.5 2.9 %collective-permute-start.4 = (bf16[2,256,128]{2,1,0:T(8,128)(2,1)S(1)}, bf16[2,256,128]{2,1,0:T(8,128)(2,1)S(1)}, u32[]{:S(2)}, u32[]{:S(2)}) collective-permute-start(bf16[2,256,128]{2,1,0:T(8,128)(2,1)S(1)} %shard_map.70.own), channel_id=1, source_target_pairs={{0,32},{1,33},{2,34},{3,35},{4,36},{5,37},{6,38},{7,39},{8,40},{9,... | collective-permute-start | bytes 393224 | tf_op jit(solution)/shard_map/ppermute | solution.py:33
  22.4 2.3 %shard_map.71.refs_0_ = bf16[512,4096]{1,0:T(8,128)(2,1)S(1)} custom-call(bf16[512,8192]{1,0:T(8,128)(2,1)} %bitcast.16), custom_call_target="tpu_custom_call" | custom-call | bytes 8388608 | tf_op jit(solution)/shard_map/pallas_call | solution.py:151
  24.7 0.2 collective-permute-done.4.other
  25.0 0.3 collective-permute-start.6
  25.3 2.5 %collective-permute-start.7 = (bf16[4,256,128]{2,1,0:T(8,128)(2,1)S(1)}, bf16[4,256,128]{2,1,0:T(8,128)(2,1)S(1)}, u32[]{:S(2)}, u32[]{:S(2)}) collective-permute-start(bf16[4,256,128]{2,1,0:T(8,128)(2,1)S(1)} %shard_map.72.own), channel_id=1, source_target_pairs={{0,28},{1,29},{2,194},{3,195},{4,0},{5,1},{6,198},{7,199},{8,4},{9... | collective-permute-start | bytes 786440 | tf_op jit(solution)/shard_map/ppermute | solution.py:33
  27.7 0.3 collective-permute-start.8
  28.0 0.0 collective-permute-done.5.tokens
  28.0 0.8 %shard_map.73.refs_1_.refs_0_ = bf16[512,4096]{1,0:T(8,128)(2,1)S(1)} custom-call(bf16[512,8192]{1,0:T(8,128)(2,1)S(1)} %collective-permute-done.5.tokens), custom_call_target="tpu_custom_call" | custom-call | bytes 8388608 | tf_op jit(solution)/shard_map/pallas_call | solution.py:151
  28.8 2.7 %collective-permute-done.6.one = bf16[4,256,128]{2,1,0:T(8,128)(2,1)S(1)} collective-permute-done((bf16[4,256,128]{2,1,0:T(8,128)(2,1)S(1)}, bf16[4,256,128]{2,1,0:T(8,128)(2,1)S(1)}, u32[]{:S(2)}, u32[]{:S(2)}) %collective-permute-start.6) | collective-permute-done | bytes 262176 | tf_op jit(solution)/shard_map/ppermute | solution.py:33
  31.5 2.4 %collective-permute-done.7.two = bf16[4,256,128]{2,1,0:T(8,128)(2,1)S(1)} collective-permute-done((bf16[4,256,128]{2,1,0:T(8,128)(2,1)S(1)}, bf16[4,256,128]{2,1,0:T(8,128)(2,1)S(1)}, u32[]{:S(2)}, u32[]{:S(2)}) %collective-permute-start.7) | collective-permute-done | bytes 262176 | tf_op jit(solution)/shard_map/ppermute | solution.py:33
  33.9 0.7 %collective-permute-done.8.three = bf16[4,256,128]{2,1,0:T(8,128)(2,1)S(1)} collective-permute-done((bf16[4,256,128]{2,1,0:T(8,128)(2,1)S(1)}, bf16[4,256,128]{2,1,0:T(8,128)(2,1)S(1)}, u32[]{:S(2)}, u32[]{:S(2)}) %collective-permute-start.8) | collective-permute-done | bytes 262176 | tf_op jit(solution)/shard_map/ppermute | solution.py:33
  34.6 0.1 shard_map.74
  34.7 0.5 collective-permute-start.9
  35.2 3.4 %collective-permute-start.10 = (bf16[8,256,128]{2,1,0:T(8,128)(2,1)S(1)}, bf16[8,256,128]{2,1,0:T(8,128)(2,1)S(1)}, u32[]{:S(2)}, u32[]{:S(2)}) collective-permute-start(bf16[8,256,128]{2,1,0:T(8,128)(2,1)S(1)} %get-tuple-element.35.refs_3_), channel_id=1, source_target_pairs={{0,192},{1,193},{2,30},{3,31},{4,196},{5,197},{6,2},{7,3},{8,200},... | collective-permute-start | bytes 1572872 | tf_op jit(solution)/shard_map/ppermute | solution.py:33
  38.6 1.4 %collective-permute-start.13 = (bf16[8,256,128]{2,1,0:T(8,128)(2,1)S(1)}, bf16[8,256,128]{2,1,0:T(8,128)(2,1)S(1)}, u32[]{:S(2)}, u32[]{:S(2)}) collective-permute-start(bf16[8,256,128]{2,1,0:T(8,128)(2,1)S(1)} %get-tuple-element.34.refs_2_), channel_id=1, source_target_pairs={{0,192},{1,193},{2,30},{3,31},{4,196},{5,197},{6,2},{7,3},{8,200},... | collective-permute-start | bytes 1572872 | tf_op jit(solution)/shard_map/ppermute | solution.py:33
  40.0 0.1 collective-permute-start.14
  40.0 1.4 %shard_map.75 = (f32[512,512]{1,0:T(8,128)S(1)}, f32[512,512]{1,0:T(8,128)S(1)}) custom-call(bf16[512,4096]{1,0:T(8,128)(2,1)S(1)} %shard_map.71.refs_0_, bf16[512,4096]{1,0:T(8,128)(2,1)S(1)} %shard_map.73.refs_1_.refs_0_, bf16[8,256,128]{2,1,0:T(8,128)(2,1)S(1)} %get-tuple-element.34.refs_2_, bf16[8,256,128]{2,1,0:T(8,128)(2,1)S(1)} %get-tuple-element.35.refs_3_), custom_call_target="tpu_custom_call" | custom-call | flops 1073741824 | bytes 2097152 | tf_op jit(solution)/shard_map/pallas_call | solution.py:199
  41.5 5.6 %collective-permute-done.9.refs_2_ = bf16[8,256,128]{2,1,0:T(8,128)(2,1)S(1)} collective-permute-done((bf16[8,256,128]{2,1,0:T(8,128)(2,1)S(1)}, bf16[8,256,128]{2,1,0:T(8,128)(2,1)S(1)}, u32[]{:S(2)}, u32[]{:S(2)}) %collective-permute-start.9) | collective-permute-done | bytes 524320 | tf_op jit(solution)/shard_map/ppermute | solution.py:33
  47.0 0.0 collective-permute-done.10.refs_5_
  47.0 0.3 collective-permute-start.11
  47.3 2.4 %collective-permute-start.12 = (bf16[8,256,128]{2,1,0:T(8,128)(2,1)S(1)}, bf16[8,256,128]{2,1,0:T(8,128)(2,1)S(1)}, u32[]{:S(2)}, u32[]{:S(2)}) collective-permute-start(bf16[8,256,128]{2,1,0:T(8,128)(2,1)S(1)} %collective-permute-done.10.refs_5_), channel_id=1, source_target_pairs={{0,192},{1,193},{2,30},{3,31},{4,196},{5,197},{6,2},{7,3},{8,200},... | collective-permute-start | bytes 1572872 | tf_op jit(solution)/shard_map/ppermute | solution.py:33
  49.7 2.2 %collective-permute-done.13.refs_3_ = bf16[8,256,128]{2,1,0:T(8,128)(2,1)S(1)} collective-permute-done((bf16[8,256,128]{2,1,0:T(8,128)(2,1)S(1)}, bf16[8,256,128]{2,1,0:T(8,128)(2,1)S(1)}, u32[]{:S(2)}, u32[]{:S(2)}) %collective-permute-start.13) | collective-permute-done | bytes 524320 | tf_op jit(solution)/shard_map/ppermute | solution.py:33
  52.0 0.7 %collective-permute-done.14.refs_4_ = bf16[8,256,128]{2,1,0:T(8,128)(2,1)S(1)} collective-permute-done((bf16[8,256,128]{2,1,0:T(8,128)(2,1)S(1)}, bf16[8,256,128]{2,1,0:T(8,128)(2,1)S(1)}, u32[]{:S(2)}, u32[]{:S(2)}) %collective-permute-start.14) | collective-permute-done | bytes 524320 | tf_op jit(solution)/shard_map/ppermute | solution.py:33
  52.7 2.3 %shard_map.76 = (f32[512,512]{1,0:T(8,128)S(1)}, f32[512,512]{1,0:T(8,128)S(1)}) custom-call(bf16[512,4096]{1,0:T(8,128)(2,1)S(1)} %shard_map.71.refs_0_, bf16[512,4096]{1,0:T(8,128)(2,1)S(1)} %shard_map.73.refs_1_.refs_0_, bf16[8,256,128]{2,1,0:T(8,128)(2,1)S(1)} %collective-permute-done.9.refs_2_, ...), custom_call_target="tpu_custom_call" | custom-call | flops 2147483648 | bytes 4194304 | tf_op jit(solution)/shard_map/pallas_call | solution.py:199
  55.0 3.3 %collective-permute-done.11.refs_1_ = bf16[8,256,128]{2,1,0:T(8,128)(2,1)S(1)} collective-permute-done((bf16[8,256,128]{2,1,0:T(8,128)(2,1)S(1)}, bf16[8,256,128]{2,1,0:T(8,128)(2,1)S(1)}, u32[]{:S(2)}, u32[]{:S(2)}) %collective-permute-start.11) | collective-permute-done | bytes 524320 | tf_op jit(solution)/shard_map/ppermute | solution.py:33
  58.3 0.0 collective-permute-done.12.refs_2_
  58.3 0.7 %shard_map.78 = bf16[512,512]{1,0:T(8,128)(2,1)S(1)} custom-call(bf16[512,4096]{1,0:T(8,128)(2,1)S(1)} %shard_map.73.refs_1_.refs_0_, bf16[8,256,128]{2,1,0:T(8,128)(2,1)S(1)} %collective-permute-done.11.refs_1_, bf16[8,256,128]{2,1,0:T(8,128)(2,1)S(1)} %collective-permute-done.12.refs_2_, f32[512,512]{1,0:T(8,128)S(1)} %get-tuple-element.44.refs_3_), custom_call_target="tpu_custom_call" | custom-call | flops 536870912 | bytes 1048576 | tf_op jit(solution)/shard_map/pallas_call | solution.py:199
  59.0 6.4 %collective-permute-start.15 = (bf16[512,512]{1,0:T(8,128)(2,1)S(1)}, bf16[512,512]{1,0:T(8,128)(2,1)S(1)}, u32[]{:S(2)}, u32[]{:S(2)}) collective-permute-start(bf16[512,512]{1,0:T(8,128)(2,1)S(1)} %shard_map.78), channel_id=1, source_target_pairs={{0,2},{1,3},{2,0},{3,1},{4,6},{5,7},{6,4},{7,5},{8,10},{9,11},{10,... | collective-permute-start | bytes 1572872 | tf_op jit(solution)/shard_map/ppermute | solution.py:33
  65.4 0.8 %shard_map.79 = (f32[256,128]{1,0:T(8,128)}, f32[256,128]{1,0:T(8,128)}) custom-call(bf16[256,128]{1,0:T(8,128)(2,1)S(1)} %get-tuple-element.25.own, bf16[256,128]{1,0:T(8,128)(2,1)S(1)} %collective-permute-done.one, bf16[256,128]{1,0:T(8,128)(2,1)S(1)} %collective-permute-done.1.two, bf16[256,128]{1,0:T(8,128)(2,1)S(1)} %collective-permute-done.2.three, ...), custom_call_target="tpu_custom_call" | custom-call | bytes 1048576 | tf_op jit(solution)/shard_map/pallas_call | solution.py:219
  66.2 0.7 %shard_map.77 = f32[512,512]{1,0:T(8,128)S(1)} custom-call(bf16[512,4096]{1,0:T(8,128)(2,1)S(1)} %shard_map.71.refs_0_, bf16[8,256,128]{2,1,0:T(8,128)(2,1)S(1)} %collective-permute-done.11.refs_1_, bf16[8,256,128]{2,1,0:T(8,128)(2,1)S(1)} %collective-permute-done.12.refs_2_, f32[512,512]{1,0:T(8,128)S(1)} %get-tuple-element.43.refs_3_), custom_call_target="tpu_custom_call" | custom-call | flops 536870912 | bytes 1048576 | tf_op jit(solution)/shard_map/pallas_call | solution.py:199
  66.9 0.1 collective-permute-done.15
  67.0 1.0 %fusion = bf16[1,512,512]{2,1,0:T(8,128)(2,1)} fusion(f32[512,512]{1,0:T(8,128)S(1)} %shard_map.77, bf16[512,512]{1,0:T(8,128)(2,1)S(1)} %collective-permute-done.15), kind=kLoop, calls=%fused_computation.1 | loop fusion | flops 786432 | bytes 2097152 | tf_op jit(solution)/shard_map/broadcast_in_dim | solution.py:240
  (4 shorter events, 0.1 us)
Async XLA Ops:
  0.6 27.4 %collective-permute-start.5 = (bf16[512,8192]{1,0:T(8,128)(2,1)}, bf16[512,8192]{1,0:T(8,128)(2,1)S(1)}, u32[]{:S(2)}, u32[]{:S(2)}) collective-permute-start(bf16[512,8192]{1,0:T(8,128)(2,1)} %bitcast.15), channel_id=1, source_target_pairs={{0,2},{1,3},{2,0},{3,1},{4,6},{5,7},{6,4},{7,5},{8,10},{9,11},{10,... | collective-permute-start | bytes 25165832 | tf_op jit(solution)/shard_map/ppermute | solution.py:33
  4.0 0.9 %copy-start = (bf16[1,256,512]{2,1,0:T(8,128)(2,1)S(1)}, bf16[1,256,512]{2,1,0:T(8,128)(2,1)}, u32[]{:S(2)}) copy-start(bf16[1,256,512]{2,1,0:T(8,128)(2,1)} %param.5) | copy-start | bytes 786436
  5.0 5.0 %collective-permute-start = (bf16[256,128]{1,0:T(8,128)(2,1)S(1)}, bf16[256,128]{1,0:T(8,128)(2,1)S(1)}, u32[]{:S(2)}, u32[]{:S(2)}) collective-permute-start(bf16[256,128]{1,0:T(8,128)(2,1)S(1)} %get-tuple-element.26), channel_id=1, source_target_pairs={{0,64},{1,65},{2,66},{3,67},{4,68},{5,69},{6,70},{7,71},{8,72},{9,... | collective-permute-start | bytes 196616 | tf_op jit(solution)/shard_map/ppermute | solution.py:33
  5.1 5.5 %collective-permute-start.1 = (bf16[256,128]{1,0:T(8,128)(2,1)S(1)}, bf16[256,128]{1,0:T(8,128)(2,1)S(1)}, u32[]{:S(2)}, u32[]{:S(2)}) collective-permute-start(bf16[256,128]{1,0:T(8,128)(2,1)S(1)} %get-tuple-element.27), channel_id=1, source_target_pairs={{0,192},{1,193},{2,194},{3,195},{4,196},{5,197},{6,198},{7,199},{8... | collective-permute-start | bytes 196616 | tf_op jit(solution)/shard_map/ppermute | solution.py:33
  7.7 4.6 %collective-permute-start.2 = (bf16[256,128]{1,0:T(8,128)(2,1)S(1)}, bf16[256,128]{1,0:T(8,128)(2,1)S(1)}, u32[]{:S(2)}, u32[]{:S(2)}) collective-permute-start(bf16[256,128]{1,0:T(8,128)(2,1)S(1)} %get-tuple-element.28), channel_id=1, source_target_pairs={{0,128},{1,129},{2,130},{3,131},{4,132},{5,133},{6,134},{7,135},{8... | collective-permute-start | bytes 196616 | tf_op jit(solution)/shard_map/ppermute | solution.py:33
  7.7 0.9 %copy-start.1 = (f32[256,1,1,128]{3,2,1,0:T(1,128)S(1)}, f32[256,1,1,128]{3,2,1,0:T(1,128)}, u32[]{:S(2)}) copy-start(f32[256,1,1,128]{3,2,1,0:T(1,128)} %param.6) | copy-start | bytes 393220
  8.6 0.9 %copy-start.2 = (f32[256,1,1,128]{3,2,1,0:T(1,128)S(1)}, f32[256,1,1,128]{3,2,1,0:T(1,128)}, u32[]{:S(2)}) copy-start(f32[256,1,1,128]{3,2,1,0:T(1,128)} %param.7) | copy-start | bytes 393220
  12.4 7.1 %collective-permute-start.3 = (bf16[256,128]{1,0:T(8,128)(2,1)S(1)}, bf16[256,128]{1,0:T(8,128)(2,1)S(1)}, u32[]{:S(2)}, u32[]{:S(2)}) collective-permute-start(bf16[256,128]{1,0:T(8,128)(2,1)S(1)} %shard_map.69.own), channel_id=1, source_target_pairs={{0,16},{1,17},{2,18},{3,19},{4,20},{5,21},{6,22},{7,23},{8,24},{9,... | collective-permute-start | bytes 196616 | tf_op jit(solution)/shard_map/ppermute | solution.py:33
  19.5 5.4 %collective-permute-start.4 = (bf16[2,256,128]{2,1,0:T(8,128)(2,1)S(1)}, bf16[2,256,128]{2,1,0:T(8,128)(2,1)S(1)}, u32[]{:S(2)}, u32[]{:S(2)}) collective-permute-start(bf16[2,256,128]{2,1,0:T(8,128)(2,1)S(1)} %shard_map.70.own), channel_id=1, source_target_pairs={{0,32},{1,33},{2,34},{3,35},{4,36},{5,37},{6,38},{7,39},{8,40},{9,... | collective-permute-start | bytes 393224 | tf_op jit(solution)/shard_map/ppermute | solution.py:33
  25.0 6.5 %collective-permute-start.6 = (bf16[4,256,128]{2,1,0:T(8,128)(2,1)S(1)}, bf16[4,256,128]{2,1,0:T(8,128)(2,1)S(1)}, u32[]{:S(2)}, u32[]{:S(2)}) collective-permute-start(bf16[4,256,128]{2,1,0:T(8,128)(2,1)S(1)} %shard_map.72.own), channel_id=1, source_target_pairs={{0,4},{1,5},{2,66},{3,67},{4,8},{5,9},{6,70},{7,71},{8,12},{9,13},... | collective-permute-start | bytes 786440 | tf_op jit(solution)/shard_map/ppermute | solution.py:33
  25.3 8.6 %collective-permute-start.7 = (bf16[4,256,128]{2,1,0:T(8,128)(2,1)S(1)}, bf16[4,256,128]{2,1,0:T(8,128)(2,1)S(1)}, u32[]{:S(2)}, u32[]{:S(2)}) collective-permute-start(bf16[4,256,128]{2,1,0:T(8,128)(2,1)S(1)} %shard_map.72.own), channel_id=1, source_target_pairs={{0,28},{1,29},{2,194},{3,195},{4,0},{5,1},{6,198},{7,199},{8,4},{9... | collective-permute-start | bytes 786440 | tf_op jit(solution)/shard_map/ppermute | solution.py:33
  27.7 6.8 %collective-permute-start.8 = (bf16[4,256,128]{2,1,0:T(8,128)(2,1)S(1)}, bf16[4,256,128]{2,1,0:T(8,128)(2,1)S(1)}, u32[]{:S(2)}, u32[]{:S(2)}) collective-permute-start(bf16[4,256,128]{2,1,0:T(8,128)(2,1)S(1)} %shard_map.72.own), channel_id=1, source_target_pairs={{0,8},{1,9},{2,130},{3,131},{4,28},{5,29},{6,134},{7,135},{8,16},{... | collective-permute-start | bytes 786440 | tf_op jit(solution)/shard_map/ppermute | solution.py:33
  34.7 12.4 %collective-permute-start.9 = (bf16[8,256,128]{2,1,0:T(8,128)(2,1)S(1)}, bf16[8,256,128]{2,1,0:T(8,128)(2,1)S(1)}, u32[]{:S(2)}, u32[]{:S(2)}) collective-permute-start(bf16[8,256,128]{2,1,0:T(8,128)(2,1)S(1)} %get-tuple-element.34.refs_2_), channel_id=1, source_target_pairs={{0,64},{1,65},{2,6},{3,7},{4,68},{5,69},{6,10},{7,11},{8,72},{9,73... | collective-permute-start | bytes 1572872 | tf_op jit(solution)/shard_map/ppermute | solution.py:33
  35.2 11.8 %collective-permute-start.10 = (bf16[8,256,128]{2,1,0:T(8,128)(2,1)S(1)}, bf16[8,256,128]{2,1,0:T(8,128)(2,1)S(1)}, u32[]{:S(2)}, u32[]{:S(2)}) collective-permute-start(bf16[8,256,128]{2,1,0:T(8,128)(2,1)S(1)} %get-tuple-element.35.refs_3_), channel_id=1, source_target_pairs={{0,192},{1,193},{2,30},{3,31},{4,196},{5,197},{6,2},{7,3},{8,200},... | collective-permute-start | bytes 1572872 | tf_op jit(solution)/shard_map/ppermute | solution.py:33
  38.6 13.4 %collective-permute-start.13 = (bf16[8,256,128]{2,1,0:T(8,128)(2,1)S(1)}, bf16[8,256,128]{2,1,0:T(8,128)(2,1)S(1)}, u32[]{:S(2)}, u32[]{:S(2)}) collective-permute-start(bf16[8,256,128]{2,1,0:T(8,128)(2,1)S(1)} %get-tuple-element.34.refs_2_), channel_id=1, source_target_pairs={{0,192},{1,193},{2,30},{3,31},{4,196},{5,197},{6,2},{7,3},{8,200},... | collective-permute-start | bytes 1572872 | tf_op jit(solution)/shard_map/ppermute | solution.py:33
  40.0 12.7 %collective-permute-start.14 = (bf16[8,256,128]{2,1,0:T(8,128)(2,1)S(1)}, bf16[8,256,128]{2,1,0:T(8,128)(2,1)S(1)}, u32[]{:S(2)}, u32[]{:S(2)}) collective-permute-start(bf16[8,256,128]{2,1,0:T(8,128)(2,1)S(1)} %get-tuple-element.35.refs_3_), channel_id=1, source_target_pairs={{0,64},{1,65},{2,6},{3,7},{4,68},{5,69},{6,10},{7,11},{8,72},{9,73... | collective-permute-start | bytes 1572872 | tf_op jit(solution)/shard_map/ppermute | solution.py:33
  47.0 11.2 %collective-permute-start.11 = (bf16[8,256,128]{2,1,0:T(8,128)(2,1)S(1)}, bf16[8,256,128]{2,1,0:T(8,128)(2,1)S(1)}, u32[]{:S(2)}, u32[]{:S(2)}) collective-permute-start(bf16[8,256,128]{2,1,0:T(8,128)(2,1)S(1)} %collective-permute-done.9.refs_2_), channel_id=1, source_target_pairs={{0,64},{1,65},{2,6},{3,7},{4,68},{5,69},{6,10},{7,11},{8,72},{9,73... | collective-permute-start | bytes 1572872 | tf_op jit(solution)/shard_map/ppermute | solution.py:33
  47.3 11.0 %collective-permute-start.12 = (bf16[8,256,128]{2,1,0:T(8,128)(2,1)S(1)}, bf16[8,256,128]{2,1,0:T(8,128)(2,1)S(1)}, u32[]{:S(2)}, u32[]{:S(2)}) collective-permute-start(bf16[8,256,128]{2,1,0:T(8,128)(2,1)S(1)} %collective-permute-done.10.refs_5_), channel_id=1, source_target_pairs={{0,192},{1,193},{2,30},{3,31},{4,196},{5,197},{6,2},{7,3},{8,200},... | collective-permute-start | bytes 1572872 | tf_op jit(solution)/shard_map/ppermute | solution.py:33
  59.0 8.0 %collective-permute-start.15 = (bf16[512,512]{1,0:T(8,128)(2,1)S(1)}, bf16[512,512]{1,0:T(8,128)(2,1)S(1)}, u32[]{:S(2)}, u32[]{:S(2)}) collective-permute-start(bf16[512,512]{1,0:T(8,128)(2,1)S(1)} %shard_map.78), channel_id=1, source_target_pairs={{0,2},{1,3},{2,0},{3,1},{4,6},{5,7},{6,4},{7,5},{8,10},{9,11},{10,... | collective-permute-start | bytes 1572872 | tf_op jit(solution)/shard_map/ppermute | solution.py:33

commit v5 on v4

--- a/solution.py
+++ b/solution.py
@@ -98,17 +98,27 @@
     anchor_new[...], momentum_new[...] = step_of(own, one, two, three, anchor, kept)
 
 
-def join_far_kernel(own, other, out):
-    _, _, z, _ = position()
+def join_pair_kernel(own, other, out):
+    _, y, z, c = position()
+    here = jnp.where(c == 0, z // 4, y)
+    out[here] = own[...]
+    out[1 - here] = other[...]
+
+
+def join_pairs_kernel(own, other, out):
+    _, y, z, c = position()
     far = z // 4
-    out[far] = own[...]
-    out[1 - far] = other[...]
-
-
-def join_y_kernel(own, other, out):
-    _, y, _, _ = position()
-    out[pl.ds(y * 2, 2)] = own[...]
-    out[pl.ds((1 - y) * 2, 2)] = other[...]
+
+    @pl.when(c == 0)
+    def _():
+        out[pl.ds(y * 2, 2)] = own[...]
+        out[pl.ds((1 - y) * 2, 2)] = other[...]
+
+    @pl.when(c == 1)
+    def _():
+        for k in range(2):
+            out[k * 2 + far] = own[k]
+            out[k * 2 + 1 - far] = other[k]
 
 
 def join_four_kernel(own, one, two, three, low, high):
@@ -212,17 +222,24 @@
     state = jax.ShapeDtypeStruct((256, 128), jnp.float32)
     own_tokens = tokens[0]
     grads = call(split_kernel, (block,) * 4, size=2**19)(pseudo_grad[0])
-    arrived = [send(grads[k + 1], along_x(step)) for k, step in enumerate(STEPS)]
+    parts = dict(zip(STEPS, grads[1:]))
+    arrived = [send(parts[step], along_x(step)) for step in (1, 2, -1)]
     other_tokens = send(own_tokens, lambda x, y, z, c: (x, y, z, c + 1))
     prepared = call(prepare_kernel, (state, state), size=2**19)(anchor.reshape(256, 128), momentum.reshape(256, 128))
     (weights,) = call(weights_kernel, (block,), size=2**19)(grads[0], *arrived, *prepared)
     anchor_new, momentum_new = call(state_kernel, (state, state), size=2**20)(grads[0], *arrived, *prepared)
-    by_far = send(weights, lambda x, y, z, c: (x, y, z + 4, c))
-    (two,) = call(join_far_kernel, (blocks(2),), size=2**18)(weights, by_far)
-    by_y = send(two, lambda x, y, z, c: (x, y + 1, z, c))
+    def over_far(x, y, z, c):
+        return x, y, z + 4, c
+
+    def over_y(x, y, z, c):
+        return x, y + 1, z, c
+
+    pair = send(weights, lambda x, y, z, c: over_far(x, y, z, c) if c == 0 else over_y(x, y, z, c))
+    (two,) = call(join_pair_kernel, (blocks(2),), size=2**18)(weights, pair)
+    pair = send(two, lambda x, y, z, c: over_y(x, y, z, c) if c == 0 else over_far(x, y, z, c))
     packed_own = pack(own_tokens, pltpu.HBM, 44 * 1024 * 1024)
     two, packed_own = lax.optimization_barrier((two, packed_own))
-    (four,) = call(join_y_kernel, (blocks(4),), size=2**19)(two, by_y)
+    (four,) = call(join_pairs_kernel, (blocks(4),), size=2**19)(two, pair)
     fours = [send(four, early(step)) for step in STEPS]
     packed_other = pack(other_tokens, pltpu.VMEM, VMEM_LIMIT)
     four, packed_other = lax.optimization_barrier((four, packed_other))

time: 68.1 us -> 67.1 us (0.985)
  waiting for transfers between devices: 22.4 us -> 21.4 us
    ppermute x16, waiting for transfers between devices: 22.4 us -> 21.4 us  [send(): return lax.ppermute(value, AXES, pairs(move))]
  transfers between devices with their start and end apart: 16 -> 16, of which waited for: 13 -> 12; matrix products, arithmetic and copies ran while one was open for 0% -> 0% of each run, Pallas kernels for 13% -> 13%
where the time goes in v5:
time: 67.1 us; the launch traced here: 67 us
  starting transfers between devices  31.7 us (47%)
  waiting for transfers between devices  21.4 us (32%)
  Pallas kernels  9.35 us (14%)
  local copies, waits for them, and re-layouts  2.76 us (4%)
  other arithmetic  0.95 us (1%)
  between operations  0.75 us (1%)
    ppermute x16, starting transfers between devices, send(): return lax.ppermute(value, AXES, pairs(move))  31.7 us
    ppermute x16, waiting for transfers between devices, send(): return lax.ppermute(value, AXES, pairs(move))  21.4 us
    pallas_call x4, Pallas kernels, product(): call(functools.partial(product_kernel, steps, sides, bool(starts)), (jax....  5.19 us
    pallas_call x2, Pallas kernels, pack(): call(pack_kernel, jax.ShapeDtypeStruct((512, 4096), jnp.bfloat16), size=2...  3.13 us
    unnamed x6, local copies, waits for them, and re-layouts  2.76 us
  transfers between devices with their start and end apart: 16, of which 12 were waited for; matrix products, arithmetic and copies ran while one was open for 0% of the time, Pallas kernels for 13%

profile of v5, /device:TPU:1, one launch (start us, length us, event | category | flops | bytes accessed | tf_op | source)
XLA Modules:
  0.0 67.0 jit_solution(11060666175875038745)
XLA Ops:
  0.6 3.3 %collective-permute-start.5 = (bf16[512,8192]{1,0:T(8,128)(2,1)}, bf16[512,8192]{1,0:T(8,128)(2,1)S(1)}, u32[]{:S(2)}, u32[]{:S(2)}) collective-permute-start(bf16[512,8192]{1,0:T(8,128)(2,1)} %bitcast.15), channel_id=1, source_target_pairs={{0,2},{1,3},{2,0},{3,1},{4,6},{5,7},{6,4},{7,5},{8,10},{9,11},{10,... | collective-permute-start | bytes 25165832 | tf_op jit(solution)/shard_map/ppermute | solution.py:33
  4.0 0.0 copy-start
  4.0 0.9 %copy-done = bf16[1,256,512]{2,1,0:T(8,128)(2,1)S(1)} copy-done((bf16[1,256,512]{2,1,0:T(8,128)(2,1)S(1)}, bf16[1,256,512]{2,1,0:T(8,128)(2,1)}, u32[]{:S(2)}) %copy-start) | copy-done | bytes 262168
  5.0 0.1 collective-permute-start
  5.1 1.9 %collective-permute-start.1 = (bf16[256,128]{1,0:T(8,128)(2,1)S(1)}, bf16[256,128]{1,0:T(8,128)(2,1)S(1)}, u32[]{:S(2)}, u32[]{:S(2)}) collective-permute-start(bf16[256,128]{1,0:T(8,128)(2,1)S(1)} %get-tuple-element.27), channel_id=1, source_target_pairs={{0,128},{1,129},{2,130},{3,131},{4,132},{5,133},{6,134},{7,135},{8... | collective-permute-start | bytes 196616 | tf_op jit(solution)/shard_map/ppermute | solution.py:33
  7.0 1.2 %collective-permute-start.2 = (bf16[256,128]{1,0:T(8,128)(2,1)S(1)}, bf16[256,128]{1,0:T(8,128)(2,1)S(1)}, u32[]{:S(2)}, u32[]{:S(2)}) collective-permute-start(bf16[256,128]{1,0:T(8,128)(2,1)S(1)} %get-tuple-element.28), channel_id=1, source_target_pairs={{0,192},{1,193},{2,194},{3,195},{4,196},{5,197},{6,198},{7,199},{8... | collective-permute-start | bytes 196616 | tf_op jit(solution)/shard_map/ppermute | solution.py:33
  8.1 0.0 copy-start.1
  8.1 0.9 %copy-done.1 = f32[256,1,1,128]{3,2,1,0:T(1,128)S(1)} copy-done((f32[256,1,1,128]{3,2,1,0:T(1,128)S(1)}, f32[256,1,1,128]{3,2,1,0:T(1,128)}, u32[]{:S(2)}) %copy-start.1) | copy-done | bytes 131096
  9.0 0.0 copy-start.2
  9.0 0.9 %copy-done.2 = f32[256,1,1,128]{3,2,1,0:T(1,128)S(1)} copy-done((f32[256,1,1,128]{3,2,1,0:T(1,128)S(1)}, f32[256,1,1,128]{3,2,1,0:T(1,128)}, u32[]{:S(2)}) %copy-start.2) | copy-done | bytes 131096
  10.0 1.4 %collective-permute-done.one = bf16[256,128]{1,0:T(8,128)(2,1)S(1)} collective-permute-done((bf16[256,128]{1,0:T(8,128)(2,1)S(1)}, bf16[256,128]{1,0:T(8,128)(2,1)S(1)}, u32[]{:S(2)}, u32[]{:S(2)}) %collective-permute-start) | collective-permute-done | bytes 65568 | tf_op jit(solution)/shard_map/ppermute | solution.py:33
  11.4 0.0 collective-permute-done.1.two
  11.4 0.2 collective-permute-done.2.three
  11.6 0.1 shard_map.69.own
  11.7 2.0 %collective-permute-start.3 = (bf16[256,128]{1,0:T(8,128)(2,1)S(1)}, bf16[256,128]{1,0:T(8,128)(2,1)S(1)}, u32[]{:S(2)}, u32[]{:S(2)}) collective-permute-start(bf16[256,128]{1,0:T(8,128)(2,1)S(1)} %shard_map.69.own), channel_id=1, source_target_pairs={{0,16},{1,17},{2,34},{3,35},{4,20},{5,21},{6,38},{7,39},{8,24},{9,... | collective-permute-start | bytes 196616 | tf_op jit(solution)/shard_map/ppermute | solution.py:33
  13.7 2.7 %collective-permute-done.3.other = bf16[256,128]{1,0:T(8,128)(2,1)S(1)} collective-permute-done((bf16[256,128]{1,0:T(8,128)(2,1)S(1)}, bf16[256,128]{1,0:T(8,128)(2,1)S(1)}, u32[]{:S(2)}, u32[]{:S(2)}) %collective-permute-start.3) | collective-permute-done | bytes 65568 | tf_op jit(solution)/shard_map/ppermute | solution.py:33
  16.4 6.0 %collective-permute-start.4 = (bf16[2,256,128]{2,1,0:T(8,128)(2,1)S(1)}, bf16[2,256,128]{2,1,0:T(8,128)(2,1)S(1)}, u32[]{:S(2)}, u32[]{:S(2)}) collective-permute-start(bf16[2,256,128]{2,1,0:T(8,128)(2,1)S(1)} %shard_map.70.own), channel_id=1, source_target_pairs={{0,32},{1,33},{2,18},{3,19},{4,36},{5,37},{6,22},{7,23},{8,40},{9,... | collective-permute-start | bytes 393224 | tf_op jit(solution)/shard_map/ppermute | solution.py:33
  22.4 2.3 %shard_map.71.refs_0_ = bf16[512,4096]{1,0:T(8,128)(2,1)S(1)} custom-call(bf16[512,8192]{1,0:T(8,128)(2,1)} %bitcast.16), custom_call_target="tpu_custom_call" | custom-call | bytes 8388608 | tf_op jit(solution)/shard_map/pallas_call | solution.py:161
  24.7 0.8 %collective-permute-done.4.other = bf16[2,256,128]{2,1,0:T(8,128)(2,1)S(1)} collective-permute-done((bf16[2,256,128]{2,1,0:T(8,128)(2,1)S(1)}, bf16[2,256,128]{2,1,0:T(8,128)(2,1)S(1)}, u32[]{:S(2)}, u32[]{:S(2)}) %collective-permute-start.4) | collective-permute-done | bytes 131104 | tf_op jit(solution)/shard_map/ppermute | solution.py:33
  25.6 0.1 collective-permute-start.6
  25.7 2.7 %collective-permute-start.7 = (bf16[4,256,128]{2,1,0:T(8,128)(2,1)S(1)}, bf16[4,256,128]{2,1,0:T(8,128)(2,1)S(1)}, u32[]{:S(2)}, u32[]{:S(2)}) collective-permute-start(bf16[4,256,128]{2,1,0:T(8,128)(2,1)S(1)} %shard_map.72.own), channel_id=1, source_target_pairs={{0,28},{1,29},{2,194},{3,195},{4,0},{5,1},{6,198},{7,199},{8,4},{9... | collective-permute-start | bytes 786440 | tf_op jit(solution)/shard_map/ppermute | solution.py:33
  28.3 0.8 %collective-permute-start.8 = (bf16[4,256,128]{2,1,0:T(8,128)(2,1)S(1)}, bf16[4,256,128]{2,1,0:T(8,128)(2,1)S(1)}, u32[]{:S(2)}, u32[]{:S(2)}) collective-permute-start(bf16[4,256,128]{2,1,0:T(8,128)(2,1)S(1)} %shard_map.72.own), channel_id=1, source_target_pairs={{0,8},{1,9},{2,130},{3,131},{4,28},{5,29},{6,134},{7,135},{8,16},{... | collective-permute-start | bytes 786440 | tf_op jit(solution)/shard_map/ppermute | solution.py:33
  29.1 0.0 collective-permute-done.5.tokens
  29.2 0.8 %shard_map.73.refs_1_.refs_0_ = bf16[512,4096]{1,0:T(8,128)(2,1)S(1)} custom-call(bf16[512,8192]{1,0:T(8,128)(2,1)S(1)} %collective-permute-done.5.tokens), custom_call_target="tpu_custom_call" | custom-call | bytes 8388608 | tf_op jit(solution)/shard_map/pallas_call | solution.py:161
  30.0 2.1 %collective-permute-done.6.one = bf16[4,256,128]{2,1,0:T(8,128)(2,1)S(1)} collective-permute-done((bf16[4,256,128]{2,1,0:T(8,128)(2,1)S(1)}, bf16[4,256,128]{2,1,0:T(8,128)(2,1)S(1)}, u32[]{:S(2)}, u32[]{:S(2)}) %collective-permute-start.6) | collective-permute-done | bytes 262176 | tf_op jit(solution)/shard_map/ppermute | solution.py:33
  32.1 2.4 %collective-permute-done.7.two = bf16[4,256,128]{2,1,0:T(8,128)(2,1)S(1)} collective-permute-done((bf16[4,256,128]{2,1,0:T(8,128)(2,1)S(1)}, bf16[4,256,128]{2,1,0:T(8,128)(2,1)S(1)}, u32[]{:S(2)}, u32[]{:S(2)}) %collective-permute-start.7) | collective-permute-done | bytes 262176 | tf_op jit(solution)/shard_map/ppermute | solution.py:33
  34.4 1.3 %collective-permute-done.8.three = bf16[4,256,128]{2,1,0:T(8,128)(2,1)S(1)} collective-permute-done((bf16[4,256,128]{2,1,0:T(8,128)(2,1)S(1)}, bf16[4,256,128]{2,1,0:T(8,128)(2,1)S(1)}, u32[]{:S(2)}, u32[]{:S(2)}) %collective-permute-start.8) | collective-permute-done | bytes 262176 | tf_op jit(solution)/shard_map/ppermute | solution.py:33
  35.7 0.1 shard_map.74
  35.8 0.1 collective-permute-start.9
  35.9 3.3 %collective-permute-start.10 = (bf16[8,256,128]{2,1,0:T(8,128)(2,1)S(1)}, bf16[8,256,128]{2,1,0:T(8,128)(2,1)S(1)}, u32[]{:S(2)}, u32[]{:S(2)}) collective-permute-start(bf16[8,256,128]{2,1,0:T(8,128)(2,1)S(1)} %get-tuple-element.35.refs_3_), channel_id=1, source_target_pairs={{0,192},{1,193},{2,30},{3,31},{4,196},{5,197},{6,2},{7,3},{8,200},... | collective-permute-start | bytes 1572872 | tf_op jit(solution)/shard_map/ppermute | solution.py:33
  39.2 1.6 %collective-permute-start.13 = (bf16[8,256,128]{2,1,0:T(8,128)(2,1)S(1)}, bf16[8,256,128]{2,1,0:T(8,128)(2,1)S(1)}, u32[]{:S(2)}, u32[]{:S(2)}) collective-permute-start(bf16[8,256,128]{2,1,0:T(8,128)(2,1)S(1)} %get-tuple-element.34.refs_2_), channel_id=1, source_target_pairs={{0,192},{1,193},{2,30},{3,31},{4,196},{5,197},{6,2},{7,3},{8,200},... | collective-permute-start | bytes 1572872 | tf_op jit(solution)/shard_map/ppermute | solution.py:33
  40.8 0.0 collective-permute-start.14
  40.8 1.4 %shard_map.75 = (f32[512,512]{1,0:T(8,128)S(1)}, f32[512,512]{1,0:T(8,128)S(1)}) custom-call(bf16[512,4096]{1,0:T(8,128)(2,1)S(1)} %shard_map.71.refs_0_, bf16[512,4096]{1,0:T(8,128)(2,1)S(1)} %shard_map.73.refs_1_.refs_0_, bf16[8,256,128]{2,1,0:T(8,128)(2,1)S(1)} %get-tuple-element.34.refs_2_, bf16[8,256,128]{2,1,0:T(8,128)(2,1)S(1)} %get-tuple-element.35.refs_3_), custom_call_target="tpu_custom_call" | custom-call | flops 1073741824 | bytes 2097152 | tf_op jit(solution)/shard_map/pallas_call | solution.py:209
  42.3 4.3 %collective-permute-done.9.refs_2_ = bf16[8,256,128]{2,1,0:T(8,128)(2,1)S(1)} collective-permute-done((bf16[8,256,128]{2,1,0:T(8,128)(2,1)S(1)}, bf16[8,256,128]{2,1,0:T(8,128)(2,1)S(1)}, u32[]{:S(2)}, u32[]{:S(2)}) %collective-permute-start.9) | collective-permute-done | bytes 524320 | tf_op jit(solution)/shard_map/ppermute | solution.py:33
  46.5 0.0 collective-permute-done.10.refs_5_
  46.5 1.0 %collective-permute-start.11 = (bf16[8,256,128]{2,1,0:T(8,128)(2,1)S(1)}, bf16[8,256,128]{2,1,0:T(8,128)(2,1)S(1)}, u32[]{:S(2)}, u32[]{:S(2)}) collective-permute-start(bf16[8,256,128]{2,1,0:T(8,128)(2,1)S(1)} %collective-permute-done.9.refs_2_), channel_id=1, source_target_pairs={{0,64},{1,65},{2,6},{3,7},{4,68},{5,69},{6,10},{7,11},{8,72},{9,73... | collective-permute-start | bytes 1572872 | tf_op jit(solution)/shard_map/ppermute | solution.py:33
  47.5 1.7 %collective-permute-start.12 = (bf16[8,256,128]{2,1,0:T(8,128)(2,1)S(1)}, bf16[8,256,128]{2,1,0:T(8,128)(2,1)S(1)}, u32[]{:S(2)}, u32[]{:S(2)}) collective-permute-start(bf16[8,256,128]{2,1,0:T(8,128)(2,1)S(1)} %collective-permute-done.10.refs_5_), channel_id=1, source_target_pairs={{0,192},{1,193},{2,30},{3,31},{4,196},{5,197},{6,2},{7,3},{8,200},... | collective-permute-start | bytes 1572872 | tf_op jit(solution)/shard_map/ppermute | solution.py:33
  49.2 2.2 %collective-permute-done.13.refs_3_ = bf16[8,256,128]{2,1,0:T(8,128)(2,1)S(1)} collective-permute-done((bf16[8,256,128]{2,1,0:T(8,128)(2,1)S(1)}, bf16[8,256,128]{2,1,0:T(8,128)(2,1)S(1)}, u32[]{:S(2)}, u32[]{:S(2)}) %collective-permute-start.13) | collective-permute-done | bytes 524320 | tf_op jit(solution)/shard_map/ppermute | solution.py:33
  51.3 0.8 %collective-permute-done.14.refs_4_ = bf16[8,256,128]{2,1,0:T(8,128)(2,1)S(1)} collective-permute-done((bf16[8,256,128]{2,1,0:T(8,128)(2,1)S(1)}, bf16[8,256,128]{2,1,0:T(8,128)(2,1)S(1)}, u32[]{:S(2)}, u32[]{:S(2)}) %collective-permute-start.14) | collective-permute-done | bytes 524320 | tf_op jit(solution)/shard_map/ppermute | solution.py:33
  52.1 2.3 %shard_map.76 = (f32[512,512]{1,0:T(8,128)S(1)}, f32[512,512]{1,0:T(8,128)S(1)}) custom-call(bf16[512,4096]{1,0:T(8,128)(2,1)S(1)} %shard_map.71.refs_0_, bf16[512,4096]{1,0:T(8,128)(2,1)S(1)} %shard_map.73.refs_1_.refs_0_, bf16[8,256,128]{2,1,0:T(8,128)(2,1)S(1)} %collective-permute-done.9.refs_2_, ...), custom_call_target="tpu_custom_call" | custom-call | flops 2147483648 | bytes 4194304 | tf_op jit(solution)/shard_map/pallas_call | solution.py:209
  54.5 3.3 %collective-permute-done.11.refs_1_ = bf16[8,256,128]{2,1,0:T(8,128)(2,1)S(1)} collective-permute-done((bf16[8,256,128]{2,1,0:T(8,128)(2,1)S(1)}, bf16[8,256,128]{2,1,0:T(8,128)(2,1)S(1)}, u32[]{:S(2)}, u32[]{:S(2)}) %collective-permute-start.11) | collective-permute-done | bytes 524320 | tf_op jit(solution)/shard_map/ppermute | solution.py:33
  57.7 0.0 collective-permute-done.12.refs_2_
  57.8 0.7 %shard_map.78 = bf16[512,512]{1,0:T(8,128)(2,1)S(1)} custom-call(bf16[512,4096]{1,0:T(8,128)(2,1)S(1)} %shard_map.73.refs_1_.refs_0_, bf16[8,256,128]{2,1,0:T(8,128)(2,1)S(1)} %collective-permute-done.11.refs_1_, bf16[8,256,128]{2,1,0:T(8,128)(2,1)S(1)} %collective-permute-done.12.refs_2_, f32[512,512]{1,0:T(8,128)S(1)} %get-tuple-element.44.refs_3_), custom_call_target="tpu_custom_call" | custom-call | flops 536870912 | bytes 1048576 | tf_op jit(solution)/shard_map/pallas_call | solution.py:209
  58.5 6.0 %collective-permute-start.15 = (bf16[512,512]{1,0:T(8,128)(2,1)S(1)}, bf16[512,512]{1,0:T(8,128)(2,1)S(1)}, u32[]{:S(2)}, u32[]{:S(2)}) collective-permute-start(bf16[512,512]{1,0:T(8,128)(2,1)S(1)} %shard_map.78), channel_id=1, source_target_pairs={{0,2},{1,3},{2,0},{3,1},{4,6},{5,7},{6,4},{7,5},{8,10},{9,11},{10,... | collective-permute-start | bytes 1572872 | tf_op jit(solution)/shard_map/ppermute | solution.py:33
  64.5 0.8 %shard_map.79 = (f32[256,128]{1,0:T(8,128)}, f32[256,128]{1,0:T(8,128)}) custom-call(bf16[256,128]{1,0:T(8,128)(2,1)S(1)} %get-tuple-element.25.own, bf16[256,128]{1,0:T(8,128)(2,1)S(1)} %collective-permute-done.one, bf16[256,128]{1,0:T(8,128)(2,1)S(1)} %collective-permute-done.1.two, bf16[256,128]{1,0:T(8,128)(2,1)S(1)} %collective-permute-done.2.three, ...), custom_call_target="tpu_custom_call" | custom-call | bytes 1048576 | tf_op jit(solution)/shard_map/pallas_call | solution.py:230
  65.3 0.7 %shard_map.77 = f32[512,512]{1,0:T(8,128)S(1)} custom-call(bf16[512,4096]{1,0:T(8,128)(2,1)S(1)} %shard_map.71.refs_0_, bf16[8,256,128]{2,1,0:T(8,128)(2,1)S(1)} %collective-permute-done.11.refs_1_, bf16[8,256,128]{2,1,0:T(8,128)(2,1)S(1)} %collective-permute-done.12.refs_2_, f32[512,512]{1,0:T(8,128)S(1)} %get-tuple-element.43.refs_3_), custom_call_target="tpu_custom_call" | custom-call | flops 536870912 | bytes 1048576 | tf_op jit(solution)/shard_map/pallas_call | solution.py:209
  66.0 0.1 collective-permute-done.15
  66.0 1.0 %fusion = bf16[1,512,512]{2,1,0:T(8,128)(2,1)} fusion(f32[512,512]{1,0:T(8,128)S(1)} %shard_map.77, bf16[512,512]{1,0:T(8,128)(2,1)S(1)} %collective-permute-done.15), kind=kLoop, calls=%fused_computation.1 | loop fusion | flops 786432 | bytes 2097152 | tf_op jit(solution)/shard_map/broadcast_in_dim | solution.py:257
  (4 shorter events, 0.1 us)
Async XLA Ops:
  0.6 28.5 %collective-permute-start.5 = (bf16[512,8192]{1,0:T(8,128)(2,1)}, bf16[512,8192]{1,0:T(8,128)(2,1)S(1)}, u32[]{:S(2)}, u32[]{:S(2)}) collective-permute-start(bf16[512,8192]{1,0:T(8,128)(2,1)} %bitcast.15), channel_id=1, source_target_pairs={{0,2},{1,3},{2,0},{3,1},{4,6},{5,7},{6,4},{7,5},{8,10},{9,11},{10,... | collective-permute-start | bytes 25165832 | tf_op jit(solution)/shard_map/ppermute | solution.py:33
  4.0 0.9 %copy-start = (bf16[1,256,512]{2,1,0:T(8,128)(2,1)S(1)}, bf16[1,256,512]{2,1,0:T(8,128)(2,1)}, u32[]{:S(2)}) copy-start(bf16[1,256,512]{2,1,0:T(8,128)(2,1)} %param.5) | copy-start | bytes 786436
  5.0 6.4 %collective-permute-start = (bf16[256,128]{1,0:T(8,128)(2,1)S(1)}, bf16[256,128]{1,0:T(8,128)(2,1)S(1)}, u32[]{:S(2)}, u32[]{:S(2)}) collective-permute-start(bf16[256,128]{1,0:T(8,128)(2,1)S(1)} %get-tuple-element.26), channel_id=1, source_target_pairs={{0,64},{1,65},{2,66},{3,67},{4,68},{5,69},{6,70},{7,71},{8,72},{9,... | collective-permute-start | bytes 196616 | tf_op jit(solution)/shard_map/ppermute | solution.py:33
  5.1 6.3 %collective-permute-start.1 = (bf16[256,128]{1,0:T(8,128)(2,1)S(1)}, bf16[256,128]{1,0:T(8,128)(2,1)S(1)}, u32[]{:S(2)}, u32[]{:S(2)}) collective-permute-start(bf16[256,128]{1,0:T(8,128)(2,1)S(1)} %get-tuple-element.27), channel_id=1, source_target_pairs={{0,128},{1,129},{2,130},{3,131},{4,132},{5,133},{6,134},{7,135},{8... | collective-permute-start | bytes 196616 | tf_op jit(solution)/shard_map/ppermute | solution.py:33
  7.0 4.7 %collective-permute-start.2 = (bf16[256,128]{1,0:T(8,128)(2,1)S(1)}, bf16[256,128]{1,0:T(8,128)(2,1)S(1)}, u32[]{:S(2)}, u32[]{:S(2)}) collective-permute-start(bf16[256,128]{1,0:T(8,128)(2,1)S(1)} %get-tuple-element.28), channel_id=1, source_target_pairs={{0,192},{1,193},{2,194},{3,195},{4,196},{5,197},{6,198},{7,199},{8... | collective-permute-start | bytes 196616 | tf_op jit(solution)/shard_map/ppermute | solution.py:33
  8.1 0.9 %copy-start.1 = (f32[256,1,1,128]{3,2,1,0:T(1,128)S(1)}, f32[256,1,1,128]{3,2,1,0:T(1,128)}, u32[]{:S(2)}) copy-start(f32[256,1,1,128]{3,2,1,0:T(1,128)} %param.6) | copy-start | bytes 393220
  9.0 0.9 %copy-start.2 = (f32[256,1,1,128]{3,2,1,0:T(1,128)S(1)}, f32[256,1,1,128]{3,2,1,0:T(1,128)}, u32[]{:S(2)}) copy-start(f32[256,1,1,128]{3,2,1,0:T(1,128)} %param.7) | copy-start | bytes 393220
  11.7 4.7 %collective-permute-start.3 = (bf16[256,128]{1,0:T(8,128)(2,1)S(1)}, bf16[256,128]{1,0:T(8,128)(2,1)S(1)}, u32[]{:S(2)}, u32[]{:S(2)}) collective-permute-start(bf16[256,128]{1,0:T(8,128)(2,1)S(1)} %shard_map.69.own), channel_id=1, source_target_pairs={{0,16},{1,17},{2,34},{3,35},{4,20},{5,21},{6,38},{7,39},{8,24},{9,... | collective-permute-start | bytes 196616 | tf_op jit(solution)/shard_map/ppermute | solution.py:33
  16.4 9.1 %collective-permute-start.4 = (bf16[2,256,128]{2,1,0:T(8,128)(2,1)S(1)}, bf16[2,256,128]{2,1,0:T(8,128)(2,1)S(1)}, u32[]{:S(2)}, u32[]{:S(2)}) collective-permute-start(bf16[2,256,128]{2,1,0:T(8,128)(2,1)S(1)} %shard_map.70.own), channel_id=1, source_target_pairs={{0,32},{1,33},{2,18},{3,19},{4,36},{5,37},{6,22},{7,23},{8,40},{9,... | collective-permute-start | bytes 393224 | tf_op jit(solution)/shard_map/ppermute | solution.py:33
  25.6 6.5 %collective-permute-start.6 = (bf16[4,256,128]{2,1,0:T(8,128)(2,1)S(1)}, bf16[4,256,128]{2,1,0:T(8,128)(2,1)S(1)}, u32[]{:S(2)}, u32[]{:S(2)}) collective-permute-start(bf16[4,256,128]{2,1,0:T(8,128)(2,1)S(1)} %shard_map.72.own), channel_id=1, source_target_pairs={{0,4},{1,5},{2,66},{3,67},{4,8},{5,9},{6,70},{7,71},{8,12},{9,13},... | collective-permute-start | bytes 786440 | tf_op jit(solution)/shard_map/ppermute | solution.py:33
  25.7 8.8 %collective-permute-start.7 = (bf16[4,256,128]{2,1,0:T(8,128)(2,1)S(1)}, bf16[4,256,128]{2,1,0:T(8,128)(2,1)S(1)}, u32[]{:S(2)}, u32[]{:S(2)}) collective-permute-start(bf16[4,256,128]{2,1,0:T(8,128)(2,1)S(1)} %shard_map.72.own), channel_id=1, source_target_pairs={{0,28},{1,29},{2,194},{3,195},{4,0},{5,1},{6,198},{7,199},{8,4},{9... | collective-permute-start | bytes 786440 | tf_op jit(solution)/shard_map/ppermute | solution.py:33
  28.3 7.4 %collective-permute-start.8 = (bf16[4,256,128]{2,1,0:T(8,128)(2,1)S(1)}, bf16[4,256,128]{2,1,0:T(8,128)(2,1)S(1)}, u32[]{:S(2)}, u32[]{:S(2)}) collective-permute-start(bf16[4,256,128]{2,1,0:T(8,128)(2,1)S(1)} %shard_map.72.own), channel_id=1, source_target_pairs={{0,8},{1,9},{2,130},{3,131},{4,28},{5,29},{6,134},{7,135},{8,16},{... | collective-permute-start | bytes 786440 | tf_op jit(solution)/shard_map/ppermute | solution.py:33
  35.8 10.7 %collective-permute-start.9 = (bf16[8,256,128]{2,1,0:T(8,128)(2,1)S(1)}, bf16[8,256,128]{2,1,0:T(8,128)(2,1)S(1)}, u32[]{:S(2)}, u32[]{:S(2)}) collective-permute-start(bf16[8,256,128]{2,1,0:T(8,128)(2,1)S(1)} %get-tuple-element.34.refs_2_), channel_id=1, source_target_pairs={{0,64},{1,65},{2,6},{3,7},{4,68},{5,69},{6,10},{7,11},{8,72},{9,73... | collective-permute-start | bytes 1572872 | tf_op jit(solution)/shard_map/ppermute | solution.py:33
  35.9 10.6 %collective-permute-start.10 = (bf16[8,256,128]{2,1,0:T(8,128)(2,1)S(1)}, bf16[8,256,128]{2,1,0:T(8,128)(2,1)S(1)}, u32[]{:S(2)}, u32[]{:S(2)}) collective-permute-start(bf16[8,256,128]{2,1,0:T(8,128)(2,1)S(1)} %get-tuple-element.35.refs_3_), channel_id=1, source_target_pairs={{0,192},{1,193},{2,30},{3,31},{4,196},{5,197},{6,2},{7,3},{8,200},... | collective-permute-start | bytes 1572872 | tf_op jit(solution)/shard_map/ppermute | solution.py:33
  39.2 12.1 %collective-permute-start.13 = (bf16[8,256,128]{2,1,0:T(8,128)(2,1)S(1)}, bf16[8,256,128]{2,1,0:T(8,128)(2,1)S(1)}, u32[]{:S(2)}, u32[]{:S(2)}) collective-permute-start(bf16[8,256,128]{2,1,0:T(8,128)(2,1)S(1)} %get-tuple-element.34.refs_2_), channel_id=1, source_target_pairs={{0,192},{1,193},{2,30},{3,31},{4,196},{5,197},{6,2},{7,3},{8,200},... | collective-permute-start | bytes 1572872 | tf_op jit(solution)/shard_map/ppermute | solution.py:33
  40.8 11.3 %collective-permute-start.14 = (bf16[8,256,128]{2,1,0:T(8,128)(2,1)S(1)}, bf16[8,256,128]{2,1,0:T(8,128)(2,1)S(1)}, u32[]{:S(2)}, u32[]{:S(2)}) collective-permute-start(bf16[8,256,128]{2,1,0:T(8,128)(2,1)S(1)} %get-tuple-element.35.refs_3_), channel_id=1, source_target_pairs={{0,64},{1,65},{2,6},{3,7},{4,68},{5,69},{6,10},{7,11},{8,72},{9,73... | collective-permute-start | bytes 1572872 | tf_op jit(solution)/shard_map/ppermute | solution.py:33
  46.5 11.2 %collective-permute-start.11 = (bf16[8,256,128]{2,1,0:T(8,128)(2,1)S(1)}, bf16[8,256,128]{2,1,0:T(8,128)(2,1)S(1)}, u32[]{:S(2)}, u32[]{:S(2)}) collective-permute-start(bf16[8,256,128]{2,1,0:T(8,128)(2,1)S(1)} %collective-permute-done.9.refs_2_), channel_id=1, source_target_pairs={{0,64},{1,65},{2,6},{3,7},{4,68},{5,69},{6,10},{7,11},{8,72},{9,73... | collective-permute-start | bytes 1572872 | tf_op jit(solution)/shard_map/ppermute | solution.py:33
  47.5 10.3 %collective-permute-start.12 = (bf16[8,256,128]{2,1,0:T(8,128)(2,1)S(1)}, bf16[8,256,128]{2,1,0:T(8,128)(2,1)S(1)}, u32[]{:S(2)}, u32[]{:S(2)}) collective-permute-start(bf16[8,256,128]{2,1,0:T(8,128)(2,1)S(1)} %collective-permute-done.10.refs_5_), channel_id=1, source_target_pairs={{0,192},{1,193},{2,30},{3,31},{4,196},{5,197},{6,2},{7,3},{8,200},... | collective-permute-start | bytes 1572872 | tf_op jit(solution)/shard_map/ppermute | solution.py:33
  58.5 7.6 %collective-permute-start.15 = (bf16[512,512]{1,0:T(8,128)(2,1)S(1)}, bf16[512,512]{1,0:T(8,128)(2,1)S(1)}, u32[]{:S(2)}, u32[]{:S(2)}) collective-permute-start(bf16[512,512]{1,0:T(8,128)(2,1)S(1)} %shard_map.78), channel_id=1, source_target_pairs={{0,2},{1,3},{2,0},{3,1},{4,6},{5,7},{6,4},{7,5},{8,10},{9,11},{10,... | collective-permute-start | bytes 1572872 | tf_op jit(solution)/shard_map/ppermute | solution.py:33
